TPU v7x, 32 devices: a whole 2x2x4 slice. The times are simulated.
32 devices in a mesh: atom: 4 (over x, core), tm: 8 (over z, y).
Axes of the slice: x: 2, y: 2, z: 4, core: 2. Of those that a mesh axis runs over, the one named last changes fastest.
Arguments:
- positions: int32 [64, 3, 8192], P('tm', None, 'atom'), may hold values from 0 to 131071, as said below
- velocity: bfloat16 [64, 3, 8192], P('tm', None, 'atom'), may hold values from -5 to 5
Outputs:
- correlation: float32 [4, 16, 32768], P(None, None, ('atom', 'tm'))
Inputs may be any that keep to these rules, and one draw needn't show every extreme that they name: `positions`: along each axis an atom's coordinate changes between consecutive frames by at most 1536 lattice points, counted modulo 131072.
All inputs are finite; a program needn't handle non-finite values.
Results may differ from a plain program's by a relative error of at most 0.00075.
Values may be sent and summed in bfloat16 or wider, within the bound.
A program may use at most 128 MiB of HBM per device.

v0:
```python
import math

import jax
import jax.numpy as jnp
from jax import lax
from jax.sharding import PartitionSpec as P

KX = 32
KY = 32
KZ = 32
LAGS = 16
LATTICE = 131072


def wave_numbers(number, offset, extent):
    counter = jnp.arange(number, dtype=jnp.int32) + offset
    return counter - extent // 2 + (counter >= extent // 2).astype(jnp.int32)


def phase_pair(coords, numbers):
    folded = numbers[None, :, None] * coords[:, None, :] % LATTICE
    angles = folded.astype(jnp.float32) * (2.0 * math.pi / LATTICE)
    return (jnp.cos(angles), jnp.sin(angles))


def operands(positions, velocity, kx_first, kx_number):
    frame_count, atom_count = (positions.shape[0], positions.shape[2])
    cos_x, sin_x = phase_pair(positions[:, 0], wave_numbers(kx_number, kx_first, KX))
    cos_y, sin_y = phase_pair(positions[:, 1], wave_numbers(KY, 0, KY))
    cos_z, sin_z = phase_pair(positions[:, 2], wave_numbers(KZ, 0, KZ))
    real_xy = cos_x[:, :, None] * cos_y[:, None] - sin_x[:, :, None] * sin_y[:, None]
    imag_xy = cos_x[:, :, None] * sin_y[:, None] + sin_x[:, :, None] * cos_y[:, None]
    left_side = jnp.concatenate([real_xy, imag_xy], 1)
    left_side = left_side.reshape(frame_count, 2 * kx_number * KY, atom_count).astype(jnp.bfloat16)
    weights = jnp.concatenate(
        [jnp.ones((frame_count, 1, atom_count), jnp.float32), velocity.astype(jnp.float32)], 1
    )
    right_side = jnp.stack(
        [cos_z[:, None] * weights[:, :, None], sin_z[:, None] * weights[:, :, None]], 2
    )
    right_side = right_side.reshape(frame_count, -1, atom_count).astype(jnp.bfloat16)
    return (left_side, right_side)


def finish(raw, row_count):
    frame_count = raw.shape[0]
    split = raw.reshape(frame_count, 2, row_count, -1, 2, KZ)
    real_part = split[:, 0, :, :, 0] - split[:, 1, :, :, 1]
    imag_part = split[:, 0, :, :, 1] + split[:, 1, :, :, 0]
    joined = jnp.stack([real_part, imag_part], 3)
    return jnp.transpose(joined, (1, 0, 2, 3, 4)).reshape(row_count, -1)


def mode_rows(positions, velocity, kx_first, kx_number):
    frame_count, atom_count = (positions.shape[0], positions.shape[2])
    atom_block = math.gcd(atom_count, 256)
    row_count = kx_number * KY
    channels = (velocity.shape[1] + 1) * 2 * KZ

    def accumulate(running, block_index):
        pos_block = lax.dynamic_slice_in_dim(positions, block_index * atom_block, atom_block, 2)
        vel_block = lax.dynamic_slice_in_dim(velocity, block_index * atom_block, atom_block, 2)
        left_side, right_side = operands(pos_block, vel_block, kx_first, kx_number)
        product = jnp.einsum(
            "fra,fca->frc", left_side, right_side, preferred_element_type=jnp.float32
        )
        return (running + product, None)

    initial = jnp.zeros((frame_count, 2 * row_count, channels), jnp.float32)
    running = lax.scan(accumulate, initial, jnp.arange(atom_count // atom_block, dtype=jnp.int32))[
        0
    ]
    return finish(running, row_count)


def lag_sum(anchors, partners, divisor):
    product = (anchors * partners).reshape(anchors.shape[0], anchors.shape[1], -1, 2, KZ)
    return jnp.sum(product, axis=(1, 3)) / divisor


def arrange(results):
    stacked = jnp.stack(results)
    return jnp.transpose(stacked, (2, 0, 1, 3)).reshape(stacked.shape[2], LAGS, -1)


def per_device(positions, velocity):
    atom_ways = lax.axis_size("atom")
    time_ways = lax.axis_size("tm")
    frame_count = positions.shape[0]
    atom_local = positions.shape[2]
    row_count = KX * KY // atom_ways
    channels = (velocity.shape[1] + 1) * 2 * KZ
    local_modes = lax.psum_scatter(
        mode_rows(positions, velocity, jnp.int32(0) // KY, row_count * lax.axis_size("atom") // KY),
        "atom",
        scatter_dimension=0,
        tiled=True,
    )
    local_modes = local_modes.reshape(row_count, frame_count, channels)
    total_frames = frame_count * time_ways
    atom_total = atom_local * atom_ways
    results = []
    series = lax.all_to_all(local_modes, "tm", split_axis=0, concat_axis=1, tiled=True)
    for lag_index in range(LAGS):
        divisor = atom_total * (total_frames - lag_index)
        results.append(
            lag_sum(series[:, : total_frames - lag_index], series[:, lag_index:], divisor)
        )
    return arrange(results)


def solution(mesh):
    in_specs = (P("tm", None, "atom"), P("tm", None, "atom"))
    out_specs = P(None, None, ("atom", "tm"))
    return jax.shard_map(
        per_device, mesh=mesh, in_specs=in_specs, out_specs=out_specs, check_vma=False
    )
```

profile of v0, /device:TPU:0, one launch (start us, length us, event | category | flops | bytes accessed | tf_op | source)
XLA Modules:
  0.0 498.3 jit_solution(5706266559983027130)
XLA Ops:
  6.5 271.4 %while.14 = (s32[]{:T(128)}, f32[8,2048,256]{2,1,0:T(8,128)}, s32[8]{0:T(128)S(1)}, s32[8,3,2048]{2,0,1:T(8,128)}, bf16[8,3,2048]{2,0,1:T(8,128)(2,1)}, /*index=...) while((s32[]{:T(128)}, f32[8,2048,256]{2,1,0:T(8,128)}, s32[8]{0:T(128)S(1)}, ...), condition=%wide.region_1.2_spmd.clone, body=%wide.region_0.1_spmd.clone.sunk | while | flops 2181177600 | bytes 74650080 | solution.py:70
  6.5 0.7 dynamic_slice.29
  7.9 0.7 constant_dynamic-slice_fusion.2
  8.7 0.7 dynamic-slice_bitcast_fusion.4
  9.4 3.1 fusion.76
  12.9 4.5 subtract_convert_fusion.2
  17.4 7.4 %pad_maximum_fusion.4 = bf16[8,64,32,256]{3,2,1,0:T(8,128)(2,1)} fusion(bf16[8,32,32,256]{3,2,1,0:T(8,128)(2,1)} %get-tuple-element.224, bf16[8,32,32,256]{3,2,1,0:T(8,128)(2,1)} %get-tuple-element.225), kind=kLoop, calls=%fused_computation.1.clone.1 | loop fusion | flops 4194304 | bytes 16777216 | tf_op jit(solution)/shard_map/while/body/eval_jaxpr/concatenate | solution.py:33
  24.8 11.5 %select_add_fusion.2 = f32[8,2048,256]{2,1,0:T(8,128)} fusion(f32[8,2048,256]{2,1,0:T(8,128)} %get-tuple-element.242, pred[]{:T(512)S(6)} %compare.12, bf16[8,2048,256]{2,1,0:T(8,128)(2,1)} %bitcast.119, bf16[8,256,256]{2,1,0:T(8,128)(2,1)S(1)} %bitcast.120), kind=kOutput, calls=%fused_computation.clone.1 | convolution fusion | flops 2155872256 | bytes 42991616 | tf_op jit(solution)/shard_map/while/body/eval_jaxpr/fra,fca->frc/dot_general | solution.py:64
  36.3 0.7 dynamic_slice.29
  37.7 0.7 constant_dynamic-slice_fusion.2
  38.4 0.7 dynamic-slice_bitcast_fusion.4
  39.2 3.1 fusion.76
  42.7 4.5 subtract_convert_fusion.2
  47.2 7.4 %pad_maximum_fusion.4 = bf16[8,64,32,256]{3,2,1,0:T(8,128)(2,1)} fusion(bf16[8,32,32,256]{3,2,1,0:T(8,128)(2,1)} %get-tuple-element.224, bf16[8,32,32,256]{3,2,1,0:T(8,128)(2,1)} %get-tuple-element.225), kind=kLoop, calls=%fused_computation.1.clone.1 | loop fusion | flops 4194304 | bytes 16777216 | tf_op jit(solution)/shard_map/while/body/eval_jaxpr/concatenate | solution.py:33
  54.6 16.3 %select_add_fusion.2 = f32[8,2048,256]{2,1,0:T(8,128)} fusion(f32[8,2048,256]{2,1,0:T(8,128)} %get-tuple-element.242, pred[]{:T(512)S(6)} %compare.12, bf16[8,2048,256]{2,1,0:T(8,128)(2,1)} %bitcast.119, bf16[8,256,256]{2,1,0:T(8,128)(2,1)S(1)} %bitcast.120), kind=kOutput, calls=%fused_computation.clone.1 | convolution fusion | flops 2155872256 | bytes 42991616 | tf_op jit(solution)/shard_map/while/body/eval_jaxpr/fra,fca->frc/dot_general | solution.py:64
  70.8 0.7 dynamic_slice.29
  72.2 0.7 constant_dynamic-slice_fusion.2
  72.9 0.7 dynamic-slice_bitcast_fusion.4
  73.7 3.1 fusion.76
  77.2 4.5 subtract_convert_fusion.2
  81.7 7.4 %pad_maximum_fusion.4 = bf16[8,64,32,256]{3,2,1,0:T(8,128)(2,1)} fusion(bf16[8,32,32,256]{3,2,1,0:T(8,128)(2,1)} %get-tuple-element.224, bf16[8,32,32,256]{3,2,1,0:T(8,128)(2,1)} %get-tuple-element.225), kind=kLoop, calls=%fused_computation.1.clone.1 | loop fusion | flops 4194304 | bytes 16777216 | tf_op jit(solution)/shard_map/while/body/eval_jaxpr/concatenate | solution.py:33
  89.1 16.2 %select_add_fusion.2 = f32[8,2048,256]{2,1,0:T(8,128)} fusion(f32[8,2048,256]{2,1,0:T(8,128)} %get-tuple-element.242, pred[]{:T(512)S(6)} %compare.12, bf16[8,2048,256]{2,1,0:T(8,128)(2,1)} %bitcast.119, bf16[8,256,256]{2,1,0:T(8,128)(2,1)S(1)} %bitcast.120), kind=kOutput, calls=%fused_computation.clone.1 | convolution fusion | flops 2155872256 | bytes 42991616 | tf_op jit(solution)/shard_map/while/body/eval_jaxpr/fra,fca->frc/dot_general | solution.py:64
  105.3 0.7 dynamic_slice.29
  106.7 0.7 constant_dynamic-slice_fusion.2
  107.5 0.7 dynamic-slice_bitcast_fusion.4
  108.2 3.1 fusion.76
  111.7 4.5 subtract_convert_fusion.2
  116.2 7.4 %pad_maximum_fusion.4 = bf16[8,64,32,256]{3,2,1,0:T(8,128)(2,1)} fusion(bf16[8,32,32,256]{3,2,1,0:T(8,128)(2,1)} %get-tuple-element.224, bf16[8,32,32,256]{3,2,1,0:T(8,128)(2,1)} %get-tuple-element.225), kind=kLoop, calls=%fused_computation.1.clone.1 | loop fusion | flops 4194304 | bytes 16777216 | tf_op jit(solution)/shard_map/while/body/eval_jaxpr/concatenate | solution.py:33
  123.6 16.2 %select_add_fusion.2 = f32[8,2048,256]{2,1,0:T(8,128)} fusion(f32[8,2048,256]{2,1,0:T(8,128)} %get-tuple-element.242, pred[]{:T(512)S(6)} %compare.12, bf16[8,2048,256]{2,1,0:T(8,128)(2,1)} %bitcast.119, bf16[8,256,256]{2,1,0:T(8,128)(2,1)S(1)} %bitcast.120), kind=kOutput, calls=%fused_computation.clone.1 | convolution fusion | flops 2155872256 | bytes 42991616 | tf_op jit(solution)/shard_map/while/body/eval_jaxpr/fra,fca->frc/dot_general | solution.py:64
  141.2 0.7 constant_dynamic-slice_fusion.2
  142.0 0.7 dynamic-slice_bitcast_fusion.4
  142.7 3.1 fusion.76
  146.2 4.5 subtract_convert_fusion.2
  150.7 7.4 %pad_maximum_fusion.4 = bf16[8,64,32,256]{3,2,1,0:T(8,128)(2,1)} fusion(bf16[8,32,32,256]{3,2,1,0:T(8,128)(2,1)} %get-tuple-element.224, bf16[8,32,32,256]{3,2,1,0:T(8,128)(2,1)} %get-tuple-element.225), kind=kLoop, calls=%fused_computation.1.clone.1 | loop fusion | flops 4194304 | bytes 16777216 | tf_op jit(solution)/shard_map/while/body/eval_jaxpr/concatenate | solution.py:33
  158.1 16.2 %select_add_fusion.2 = f32[8,2048,256]{2,1,0:T(8,128)} fusion(f32[8,2048,256]{2,1,0:T(8,128)} %get-tuple-element.242, pred[]{:T(512)S(6)} %compare.12, bf16[8,2048,256]{2,1,0:T(8,128)(2,1)} %bitcast.119, bf16[8,256,256]{2,1,0:T(8,128)(2,1)S(1)} %bitcast.120), kind=kOutput, calls=%fused_computation.clone.1 | convolution fusion | flops 2155872256 | bytes 42991616 | tf_op jit(solution)/shard_map/while/body/eval_jaxpr/fra,fca->frc/dot_general | solution.py:64
  175.7 0.7 constant_dynamic-slice_fusion.2
  176.5 0.7 dynamic-slice_bitcast_fusion.4
  177.2 3.1 fusion.76
  180.7 4.5 subtract_convert_fusion.2
  185.2 7.4 %pad_maximum_fusion.4 = bf16[8,64,32,256]{3,2,1,0:T(8,128)(2,1)} fusion(bf16[8,32,32,256]{3,2,1,0:T(8,128)(2,1)} %get-tuple-element.224, bf16[8,32,32,256]{3,2,1,0:T(8,128)(2,1)} %get-tuple-element.225), kind=kLoop, calls=%fused_computation.1.clone.1 | loop fusion | flops 4194304 | bytes 16777216 | tf_op jit(solution)/shard_map/while/body/eval_jaxpr/concatenate | solution.py:33
  192.6 16.2 %select_add_fusion.2 = f32[8,2048,256]{2,1,0:T(8,128)} fusion(f32[8,2048,256]{2,1,0:T(8,128)} %get-tuple-element.242, pred[]{:T(512)S(6)} %compare.12, bf16[8,2048,256]{2,1,0:T(8,128)(2,1)} %bitcast.119, bf16[8,256,256]{2,1,0:T(8,128)(2,1)S(1)} %bitcast.120), kind=kOutput, calls=%fused_computation.clone.1 | convolution fusion | flops 2155872256 | bytes 42991616 | tf_op jit(solution)/shard_map/while/body/eval_jaxpr/fra,fca->frc/dot_general | solution.py:64
  208.9 0.7 dynamic_slice.29
  210.3 0.7 constant_dynamic-slice_fusion.2
  211.0 0.7 dynamic-slice_bitcast_fusion.4
  211.7 3.1 fusion.76
  215.3 4.5 subtract_convert_fusion.2
  219.7 7.4 %pad_maximum_fusion.4 = bf16[8,64,32,256]{3,2,1,0:T(8,128)(2,1)} fusion(bf16[8,32,32,256]{3,2,1,0:T(8,128)(2,1)} %get-tuple-element.224, bf16[8,32,32,256]{3,2,1,0:T(8,128)(2,1)} %get-tuple-element.225), kind=kLoop, calls=%fused_computation.1.clone.1 | loop fusion | flops 4194304 | bytes 16777216 | tf_op jit(solution)/shard_map/while/body/eval_jaxpr/concatenate | solution.py:33
  227.2 16.2 %select_add_fusion.2 = f32[8,2048,256]{2,1,0:T(8,128)} fusion(f32[8,2048,256]{2,1,0:T(8,128)} %get-tuple-element.242, pred[]{:T(512)S(6)} %compare.12, bf16[8,2048,256]{2,1,0:T(8,128)(2,1)} %bitcast.119, bf16[8,256,256]{2,1,0:T(8,128)(2,1)S(1)} %bitcast.120), kind=kOutput, calls=%fused_computation.clone.1 | convolution fusion | flops 2155872256 | bytes 42991616 | tf_op jit(solution)/shard_map/while/body/eval_jaxpr/fra,fca->frc/dot_general | solution.py:64
  244.8 0.7 constant_dynamic-slice_fusion.2
  245.5 0.7 dynamic-slice_bitcast_fusion.4
  246.3 3.1 fusion.76
  249.8 4.5 subtract_convert_fusion.2
  254.3 7.4 %pad_maximum_fusion.4 = bf16[8,64,32,256]{3,2,1,0:T(8,128)(2,1)} fusion(bf16[8,32,32,256]{3,2,1,0:T(8,128)(2,1)} %get-tuple-element.224, bf16[8,32,32,256]{3,2,1,0:T(8,128)(2,1)} %get-tuple-element.225), kind=kLoop, calls=%fused_computation.1.clone.1 | loop fusion | flops 4194304 | bytes 16777216 | tf_op jit(solution)/shard_map/while/body/eval_jaxpr/concatenate | solution.py:33
  261.7 16.2 %select_add_fusion.2 = f32[8,2048,256]{2,1,0:T(8,128)} fusion(f32[8,2048,256]{2,1,0:T(8,128)} %get-tuple-element.242, pred[]{:T(512)S(6)} %compare.12, bf16[8,2048,256]{2,1,0:T(8,128)(2,1)} %bitcast.119, bf16[8,256,256]{2,1,0:T(8,128)(2,1)S(1)} %bitcast.120), kind=kOutput, calls=%fused_computation.clone.1 | convolution fusion | flops 2155872256 | bytes 42991616 | tf_op jit(solution)/shard_map/while/body/eval_jaxpr/fra,fca->frc/dot_general | solution.py:64
  277.9 16.4 %copy.27 = f32[8,2048,256]{1,2,0:T(8,128)} copy(f32[8,2048,256]{2,1,0:T(8,128)} %get-tuple-element.102) | data formatting | bytes 33554432 | tf_op jit(solution)/shard_map/while | solution.py:70
  294.3 22.0 %reshape.295 = f32[8,2,1024,4,2,32]{2,1,5,4,3,0:T(2,128)} reshape(f32[8,2048,256]{1,2,0:T(8,128)} %copy.27) | data formatting | bytes 33554432 | tf_op jit(solution)/shard_map/reshape | solution.py:47
  316.3 8.1 %fusion.16 = f32[8,1024,4,1,32]{1,3,4,2,0:T(1,128)S(1)} fusion(f32[8,2,1024,4,2,32]{2,1,5,4,3,0:T(2,128)} %reshape.295), kind=kLoop, calls=%fused_computation.47 | loop fusion | flops 1048576 | bytes 12582912 | tf_op jit(solution)/shard_map/add | solution.py:49
  324.5 8.2 %fusion.18 = f32[8,1024,4,1,32]{1,3,4,2,0:T(1,128)S(1)} fusion(f32[8,2,1024,4,2,32]{2,1,5,4,3,0:T(2,128)} %reshape.295), kind=kLoop, calls=%fused_computation.50 | loop fusion | flops 1048576 | bytes 12582912 | tf_op jit(solution)/shard_map/sub | solution.py:48
  332.6 7.9 %maximum_bitcast_fusion = f32[1024,8,4,2,32]{0,3,4,2,1:T(2,128)S(1)} fusion(f32[8,1024,4,1,32]{1,3,4,2,0:T(1,128)S(1)} %fusion.16, f32[8,1024,4,1,32]{1,3,4,2,0:T(1,128)S(1)} %fusion.18), kind=kLoop, calls=%fused_computation.45 | loop fusion | flops 2097152 | bytes 16777216 | tf_op jit(solution)/shard_map/transpose | solution.py:51
  340.6 6.7 %copy.30 = f32[1024,8,4,2,32]{0,4,3,2,1:T(8,128)} copy(f32[1024,8,4,2,32]{0,3,4,2,1:T(2,128)S(1)} %maximum_bitcast_fusion) | data formatting | bytes 16777216 | tf_op jit(solution)/shard_map/transpose | solution.py:51
  347.2 74.6 %reduce-scatter.2.cloned.1.call-done = f32[256,2048]{0,1:T(8,128)} async-done(((f32[1024,2048]{0,1:T(8,128)}), f32[256,2048]{0,1:T(8,128)}) %reduce-scatter.2.cloned.1.call-update) | async-done | bytes 2097168 | tf_op jit(solution)/shard_map/reduce_scatter | solution.py:93
  421.8 2.2 copy.31
  424.0 53.6 %all_to_all.18 = f32[256,8,256]{2,1,0:T(8,128)S(1)} all-to-all(f32[256,8,256]{2,1,0:T(8,128)S(1)} %copy.31), channel_id=1, replica_groups=mesh['atom'=4,'tm'=8] {'tm'}, dimensions={0} | all-to-all | bytes 4194304 | tf_op jit(solution)/shard_map/all_to_all | solution.py:103
  490.6 0.9 copy.49
  (113 shorter events, 17.9 us)
Async XLA Ops:
  6.5 415.3 %reduce-scatter.2.cloned.1.call-start = ((), (), s32[]{:S(2)}) async-start(), calls=%async_computation.2 | async-start | bytes 10485760 | tf_op jit(solution)/shard_map/reduce_scatter | solution.py:93
Sparse Core Ops, SparseCore 0:
  347.4 74.3 reduce-scatter.1
where the time goes:
time: 500 us; the launch traced here: 498 us
  other arithmetic  157 us (31%)
  matrix products  125 us (25%)
  waiting for transfers between devices  74.6 us (15%)
  local copies, waits for them, and re-layouts  68.3 us (14%)
  blocking collectives  53.6 us (11%)
  between operations  13.8 us (3%)
  loops' own time  5.89 us (1%)
    dot_general x8, matrix products, accumulate(): jnp.einsum('fra,fca->frc', left_side, right_side, preferred_element_type=...  125 us
    reduce_scatter x1, waiting for transfers between devices, per_device(): lax.psum_scatter(mode_rows(positions, velocity, jnp.int32(0) // KY, row_c...  74.6 us
    concatenate x8, other arithmetic, operands(): left_side = jnp.concatenate([real_xy, imag_xy], 1)  59.3 us
    all_to_all x1, blocking collectives, per_device(): lax.all_to_all(local_modes, 'tm', split_axis=0, concat_axis=1, tiled=True)  53.6 us
    another operation x16, other arithmetic  38.1 us
    cos x8, other arithmetic, phase_pair(): return (jnp.cos(angles), jnp.sin(angles))  25 us
    reshape x1, local copies, waits for them, and re-layouts, finish(): split = raw.reshape(frame_count, 2, row_count, -1, 2, KZ)  22 us
    while x1, local copies, waits for them, and re-layouts, mode_rows(): lax.scan(accumulate, initial, jnp.arange(atom_count // atom_block, dtype=...  16.4 us
  transfers between devices with their start and end apart: 1, of which 1 were waited for; matrix products, arithmetic and copies ran while one was open for 0% of the time, Pallas kernels for 0%

commit v1 on v0

v1 whole, which is shorter than its diff:
```python
import functools
import math

import jax
import jax.numpy as jnp
from jax import lax
from jax.experimental import pallas as pl
from jax.experimental.pallas import tpu as pltpu
from jax.sharding import PartitionSpec as P

KX = 32
KY = 32
KZ = 32
LAGS = 16
LATTICE = 131072
QUARTER = LATTICE // 4
HALF_Z = KZ // 2
COMPS = 4
LANES = 128
VMEM = 56 * 1024 * 1024


def wave(q, extent):
    return q - extent // 2 + (1 if q >= extent // 2 else 0)


def sincos(n):
    n = jnp.bitwise_and(n, LATTICE - 1)
    quadrant = jnp.right_shift(n + QUARTER // 2, 15)
    x = (n - jnp.left_shift(quadrant, 15)).astype(jnp.float32) * (2.0 * math.pi / LATTICE)
    y = x * x
    s = y * (1.0 / 362880.0) - 1.0 / 5040.0
    s = s * y + 1.0 / 120.0
    s = s * y - 1.0 / 6.0
    s = s * y * x + x
    c = y * (1.0 / 40320.0) - 1.0 / 720.0
    c = c * y + 1.0 / 24.0
    c = c * y - 0.5
    c = c * y + 1.0
    odd = jnp.bitwise_and(quadrant, 1) == 1
    cos = jnp.where(odd, s, c)
    sin = jnp.where(odd, c, s)
    cos = jnp.where(jnp.bitwise_and(quadrant + 1, 2) == 2, -cos, cos)
    sin = jnp.where(jnp.bitwise_and(quadrant, 2) == 2, -sin, sin)
    return cos, sin


def times(a, b):
    return a[0] * b[0] - a[1] * b[1], a[0] * b[1] + a[1] * b[0]


def plus_minus(a, b):
    cc, ss, cs, sc = a[0] * b[0], a[1] * b[1], a[0] * b[1], a[1] * b[0]
    return (cc - ss, sc + cs), (cc + ss, sc - cs)


def powers(e1):
    e = {1: e1}
    e[2] = times(e1, e1)
    e[3] = times(e[2], e1)
    e[4] = times(e[2], e[2])
    e[8] = times(e[4], e[4])
    e[12], _ = plus_minus(e[8], e[4])
    for d in (1, 2, 3):
        e[8 + d], e[8 - d] = plus_minus(e[8], e[d])
    e[16] = times(e[8], e[8])
    for d in (1, 2, 3):
        _, e[16 - d] = plus_minus(e[16], e[d])
    return e


def prepare(pos, xs, yc, ys, zc, zs, lanes, frames, block, first_w, group, y_waves):
    middle = (group - 1) // 2

    def step(i, _):
        at = pl.ds(pl.multiple_of(i * block, block), block)
        n = pos(0, at)
        base = sincos((first_w + middle) * n)
        xs[0, :, at], xs[1, :, at] = base
        e1 = sincos(n)
        e = {1: e1}
        for d in range(2, group - middle):
            e[d] = times(e[d - 1], e1)
        for d in range(1, group - middle):
            xs[2 * d, :, at], xs[2 * d + 1, :, at] = e[d]
        e = powers(sincos(pos(1, at)))
        for row, w in enumerate(y_waves):
            c, s = e[abs(w)]
            yc[i, row * frames : (row + 1) * frames, :] = c
            ys[i, row * frames : (row + 1) * frames, :] = s if w > 0 else -s
        e = powers(sincos(pos(2, at)))
        for w in range(1, HALF_Z + 1):
            c, s = e[w]
            zc[i, (w - 1) * frames : w * frames, :] = c
            zs[i, (w - 1) * frames : w * frames, :] = s
        return 0

    lax.fori_loop(0, lanes // block, step, 0)


def frame_product(f, vel, xs, yc, ys, zc, zs, lanes, frames, block, group, rows):
    middle = (group - 1) // 2
    total = None
    steps = block // LANES

    def pick(ref, i):
        parts = [ref[i * steps + k, pl.ds(f, rows, stride=frames), :] for k in range(steps)]
        return jnp.concatenate(parts, 1)

    for i in range(lanes // block):
        at = pl.ds(i * block, block)
        y = (pick(yc, i), pick(ys, i))
        x = [xs[j, pl.ds(f, 1), at] for j in range(2 * (group - middle))]
        mid = times((x[0], x[1]), y)
        e = {middle: mid}
        for d in range(1, group - middle):
            up, down = plus_minus(mid, (x[2 * d], x[2 * d + 1]))
            e[middle + d] = up
            if middle - d >= 0:
                e[middle - d] = down
        left = []
        for j in range(group):
            left += [e[j][0].astype(jnp.bfloat16), e[j][1].astype(jnp.bfloat16)]
        left = jnp.concatenate(left, 0)
        right = []
        for z_ref in (zc, zs):
            z = pick(z_ref, i)
            right.append(z.astype(jnp.bfloat16))
            for a in range(COMPS - 1):
                right.append((z * vel(a, f, at)).astype(jnp.bfloat16))
        right = jnp.concatenate(right, 0)
        part = lax.dot_general(
            left, right, (((1,), (1,)), ((), ())), preferred_element_type=jnp.float32
        )
        total = part if total is None else total + part
    return total


def combine(raw, group, rows):
    lane = lax.broadcasted_iota(jnp.int32, (rows, LANES), 1)
    sign = jnp.where(lane < LANES // 2, -1.0, 1.0)
    out = []
    for j in range(group):
        re = raw[2 * j * rows : (2 * j + 1) * rows]
        im = raw[(2 * j + 1) * rows : (2 * j + 2) * rows]
        turned = pltpu.roll(im, LANES // 2, 1) * sign
        out.append(jnp.concatenate([re + turned, re - turned], 1))
    return out


def modes_kernel(dims, pos_ref, vel_ref, out_ref, xs, yc, ys, zc, zs, total):
    frames, chunk, group, rows, y_waves = dims
    first = lax.axis_index("atom") * group
    first_w = first - KX // 2 + (first >= KX // 2).astype(jnp.int32)
    total[...] = jnp.zeros_like(total)

    def chunk_step(c, _):
        base = pl.multiple_of(c * chunk, chunk)
        prepare(
            lambda a, at: pos_ref[a, :, pl.ds(pl.multiple_of(base + at.start, LANES), at.size)],
            xs, yc, ys, zc, zs, chunk, frames, LANES, first_w, group, y_waves,
        )

        def frame_step(f, _):
            total[f] += frame_product(
                f,
                lambda a, f, at: vel_ref[a, pl.ds(f, 1), pl.ds(pl.multiple_of(base + at.start, LANES), at.size)],
                xs, yc, ys, zc, zs, chunk, frames, 4 * LANES, group, rows,
            )
            return 0

        lax.fori_loop(0, frames, frame_step, 0)
        return 0

    lax.fori_loop(0, pos_ref.shape[2] // chunk, chunk_step, 0)

    def emit(f, _):
        for j, block in enumerate(combine(total[f], group, rows)):
            out_ref[j, f] = block.astype(out_ref.dtype)
        return 0

    lax.fori_loop(0, frames, emit, 0)


def modes_call(pos, vel, group, rows, y_waves):
    frames, atoms = pos.shape[1], pos.shape[2]
    chunk = math.gcd(atoms, 2048)
    kernel = functools.partial(modes_kernel, (frames, chunk, group, rows, y_waves))
    whole = pl.BlockSpec(memory_space=pltpu.VMEM)
    return pl.pallas_call(
        kernel,
        out_shape=jax.ShapeDtypeStruct((group, frames, rows, 2 * LANES), jnp.bfloat16),
        in_specs=[whole, whole],
        out_specs=whole,
        scratch_shapes=[
            pltpu.VMEM((2 * (group - (group - 1) // 2), frames, chunk), jnp.float32),
            pltpu.VMEM((chunk // LANES, rows * frames, LANES), jnp.float32),
            pltpu.VMEM((chunk // LANES, rows * frames, LANES), jnp.float32),
            pltpu.VMEM((chunk // LANES, HALF_Z * frames, LANES), jnp.float32),
            pltpu.VMEM((chunk // LANES, HALF_Z * frames, LANES), jnp.float32),
            pltpu.VMEM((frames, group * 2 * rows, LANES), jnp.float32),
        ],
        compiler_params=pltpu.CompilerParams(vmem_limit_bytes=VMEM),
        name="modes",
    )(pos, vel)


def fold_matrices():
    lane = lax.broadcasted_iota(jnp.int32, (LANES, LANES), 0)
    goal = lax.broadcasted_iota(jnp.int32, (LANES, LANES), 1)
    comp = jnp.right_shift(jnp.bitwise_and(lane, 63), 4)
    step = jnp.bitwise_and(lane, HALF_Z - 1)
    own = []
    for qz in (KZ // 2 + step, KZ // 2 - 1 - step):
        own.append(comp * KZ + qz)
    mirror = [comp * KZ + KZ - 1 - (t - comp * KZ) for t in own]
    return [[(goal == t).astype(jnp.float32).astype(jnp.bfloat16) for t in side] for side in (own, mirror)]


def exact_dot(x, matrix):
    high = x.astype(jnp.bfloat16)
    low = (x - high.astype(jnp.float32)).astype(jnp.bfloat16)
    return jnp.dot(high, matrix, preferred_element_type=jnp.float32) + jnp.dot(
        low, matrix, preferred_element_type=jnp.float32
    )


def correlate(series, wide, sums, frames, rows, atoms):
    tall = min(8, rows)
    slots = 2 * (rows // tall)

    def widen(t, _):
        block = series(t).astype(jnp.float32)
        for slot in range(slots):
            r, half = divmod(slot, 2)
            wide[slot, t] = block[r * tall : (r + 1) * tall, half * LANES : (half + 1) * LANES]
        return 0

    lax.fori_loop(0, frames, widen, 0)
    for slot in range(slots):
        r, half = divmod(slot, 2)
        window = [wide[slot, t] for t in range(LAGS)]
        acc = [None] * LAGS
        for t in range(frames):
            for lag in range(min(LAGS, frames - t)):
                product = window[0] * window[lag]
                acc[lag] = product if acc[lag] is None else acc[lag] + product
            window = window[1:]
            if t + LAGS < frames:
                window.append(wide[slot, t + LAGS])
        for lag in range(LAGS):
            sums[half, lag * rows + r * tall : lag * rows + (r + 1) * tall, :] = acc[lag] * (
                1.0 / (atoms * (frames - lag))
            )


def arrange(sums, folded, own_ref, mirror_ref, rows):
    own_fold, mirror_fold = fold_matrices()
    groups = max(1, rows // 4)
    per = rows // groups
    lane = lax.broadcasted_iota(jnp.int32, (LAGS, LANES), 1)
    block = jnp.right_shift(lane, 5)
    for fold, out_ref, flip in ((own_fold, own_ref, False), (mirror_fold, mirror_ref, True)):
        folded[...] = exact_dot(sums[0], fold[0]) + exact_dot(sums[1], fold[1])
        for g in range(groups):
            parts = [folded[pl.ds(g * per + i, LAGS, stride=rows), :] for i in range(per)]
            if flip:
                parts = parts[::-1]
            goal = groups - 1 - g if flip else g
            for c in range(COMPS):
                out = jnp.zeros((LAGS, LANES), jnp.float32)
                for i in range(per):
                    shift = ((i - c) * KZ) % LANES
                    part = parts[i] if shift == 0 else pltpu.roll(parts[i], shift, 1)
                    out = jnp.where(block == i, part, out)
                out_ref[c, :, goal * LANES : goal * LANES + LANES] = out


def correlate_kernel(dims, series_ref, own_ref, mirror_ref, wide, sums, folded):
    frames, rows, atoms = dims
    correlate(lambda t: series_ref[t], wide, sums, frames, rows, atoms)
    arrange(sums, folded, own_ref, mirror_ref, rows)


def correlate_call(series, atoms):
    frames, rows = series.shape[0], series.shape[1]
    tall = min(8, rows)
    whole = pl.BlockSpec(memory_space=pltpu.VMEM)
    out = jax.ShapeDtypeStruct((COMPS, LAGS, rows * KZ), jnp.float32)
    return pl.pallas_call(
        functools.partial(correlate_kernel, (frames, rows, atoms)),
        out_shape=(out, out),
        in_specs=[whole],
        out_specs=(whole, whole),
        scratch_shapes=[
            pltpu.VMEM((2 * (rows // tall), frames, tall, LANES), jnp.float32),
            pltpu.VMEM((2, LAGS * rows, LANES), jnp.float32),
            pltpu.VMEM((LAGS * rows, LANES), jnp.float32),
        ],
        compiler_params=pltpu.CompilerParams(vmem_limit_bytes=VMEM),
        name="correlate",
    )(series)


def per_device(positions, velocity):
    atom_ways = lax.axis_size("atom")
    time_ways = lax.axis_size("tm")
    ways = atom_ways * time_ways
    frames = positions.shape[0]
    atoms = positions.shape[2] * atom_ways
    owned = KX * KY // ways
    rows = owned // 2
    group = KX // atom_ways
    y_waves = [wave(q, KY) for q in range(KY) if q % owned >= rows]
    pos = lax.all_gather(positions, "atom", axis=2, tiled=True)
    vel = lax.all_gather(velocity, "atom", axis=2, tiled=True)
    pos = jnp.transpose(pos, (1, 0, 2))
    vel = jnp.transpose(vel, (1, 0, 2)).astype(jnp.float32)
    modes = modes_call(pos, vel, group, KY // 2, y_waves)
    split = KY // owned
    modes = modes.reshape(group, frames, split, rows, 2 * LANES)
    modes = jnp.transpose(modes, (0, 2, 1, 3, 4)).reshape(time_ways, frames, rows, 2 * LANES)
    series = lax.all_to_all(modes, "tm", split_axis=0, concat_axis=0, tiled=True)
    own, mirror = correlate_call(series.reshape(time_ways * frames, rows, 2 * LANES), atoms)
    mirror = lax.ppermute(mirror, ("atom", "tm"), [(b, ways - 1 - b) for b in range(ways)])
    return jnp.concatenate([mirror, own], 2)


def solution(mesh):
    in_specs = (P("tm", None, "atom"), P("tm", None, "atom"))
    out_specs = P(None, None, ("atom", "tm"))
    return jax.shard_map(
        per_device, mesh=mesh, in_specs=in_specs, out_specs=out_specs, check_vma=False
    )
```

time: 500 us -> 77.6 us (0.16)
  other arithmetic: 157 us -> 2.58 us
  matrix products: 125 us -> 0 us
  local copies, waits for them, and re-layouts: 68.3 us -> 0.02 us
  waiting for transfers between devices: 74.6 us -> 6.61 us
  Pallas kernels: 0 us -> 27.3 us
  blocking collectives: 53.6 us -> 38.2 us
  between operations: 13.8 us -> 0.01 us
  loops' own time: 5.89 us -> 0 us
    dot_general x8 -> x0, matrix products: 125 us -> none  [accumulate(): jnp.einsum('fra,fca->frc', left_side, right_side, preferred_element_type=...]
    reduce_scatter x1 -> x0, waiting for transfers between devices: 74.6 us -> none  [per_device(): lax.psum_scatter(mode_rows(positions, velocity, jnp.int32(0) // KY, row_c...]
    concatenate x16 -> x1, other arithmetic: 59.4 us -> 1.63 us  [per_device(): return jnp.concatenate([mirror, own], 2)]
    another operation x25 -> x0, other arithmetic: 38.9 us -> none
    all_to_all x1, blocking collectives: 53.6 us -> 20.9 us  [per_device(): lax.all_to_all(modes, 'tm', split_axis=0, concat_axis=0, tiled=True)]
    pallas_call x0 -> x2, Pallas kernels: none -> 27.3 us  [the longest x1 23.6 us: modes_call(): pl.pallas_call(kernel, out_shape=jax.ShapeDtypeStruct((group, frames, row...]
    reshape x4 -> x0, local copies, waits for them, and re-layouts: 25.6 us -> none  [the longest x1 22 us: finish(): split = raw.reshape(frame_count, 2, row_count, -1, 2, KZ)]
    cos x8 -> x0, other arithmetic: 25 us -> none  [phase_pair(): return (jnp.cos(angles), jnp.sin(angles))]
where the time goes in v1:
time: 77.6 us; the launch traced here: 77.3 us
  blocking collectives  38.2 us (49%)
  Pallas kernels  27.3 us (35%)
  waiting for transfers between devices  6.61 us (9%)
  other arithmetic  2.58 us (3%)
  starting transfers between devices  2.5 us (3%)
    pallas_call x1, Pallas kernels, modes_call(): pl.pallas_call(kernel, out_shape=jax.ShapeDtypeStruct((group, frames, row...  23.6 us
    all_to_all x1, blocking collectives, per_device(): lax.all_to_all(modes, 'tm', split_axis=0, concat_axis=0, tiled=True)  20.9 us
    all_gather x1, blocking collectives, per_device(): pos = lax.all_gather(positions, 'atom', axis=2, tiled=True)  9.16 us
    all_gather x1, blocking collectives, per_device(): vel = lax.all_gather(velocity, 'atom', axis=2, tiled=True)  8.1 us
    ppermute x1, waiting for transfers between devices, per_device(): lax.ppermute(mirror, ('atom', 'tm'), [(b, ways - 1 - b) for b in range(wa...  6.61 us
    pallas_call x1, Pallas kernels, correlate_call(): pl.pallas_call(functools.partial(correlate_kernel, (frames, rows, atoms))...  3.76 us
    ppermute x1, starting transfers between devices, per_device(): lax.ppermute(mirror, ('atom', 'tm'), [(b, ways - 1 - b) for b in range(wa...  2.5 us
    concatenate x1, other arithmetic, per_device(): return jnp.concatenate([mirror, own], 2)  1.63 us
  transfers between devices with their start and end apart: 1, of which 1 were waited for; matrix products, arithmetic and copies ran while one was open for 0% of the time, Pallas kernels for 0%

profile of v1, /device:TPU:0, one launch (start us, length us, event | category | flops | bytes accessed | tf_op | source)
XLA Modules:
  0.0 77.3 jit_solution(18129807290228823341)
XLA Ops:
  0.0 8.1 %all_gather.7 = bf16[8,3,8192]{2,0,1:T(8,128)(2,1)S(1)} all-gather(bf16[8,3,2048]{2,0,1:T(8,128)(2,1)} %param.3), channel_id=1, replica_groups=mesh['atom'=4,'tm'=8] {'atom'}, dimensions={2}, use_global_device_ids=true | all-gather | bytes 491520 | tf_op jit(solution)/shard_map/all_gather | solution.py:316
  8.1 0.0 copy-start
  8.1 1.0 %convert_bitcast_fusion.vel_ref = f32[3,8,8192]{2,1,0:T(8,128)} fusion(bf16[8,3,8192]{2,0,1:T(8,128)(2,1)S(1)} %all_gather.7), kind=kLoop, calls=%fused_computation | loop fusion | flops 196608 | bytes 1179648 | tf_op jit(solution)/shard_map/convert_element_type | solution.py:318
  9.1 0.0 copy-done
  9.1 9.2 %all_gather.6 = s32[8,3,8192]{2,0,1:T(8,128)} all-gather(s32[8,3,2048]{2,0,1:T(8,128)S(1)} %copy-done), channel_id=1, replica_groups=mesh['atom'=4,'tm'=8] {'atom'}, dimensions={2}, use_global_device_ids=true | all-gather | bytes 983040 | tf_op jit(solution)/shard_map/all_gather | solution.py:315
  18.2 23.6 %modes.1 = bf16[8,8,16,256]{3,2,1,0:T(8,128)(2,1)} custom-call(s32[3,8,8192]{2,1,0:T(8,128)} %bitcast.4, f32[3,8,8192]{2,1,0:T(8,128)} %convert_bitcast_fusion.vel_ref), custom_call_target="tpu_custom_call" | custom-call | tf_op jit(solution)/shard_map/modes/pallas_call | solution.py:190
  41.8 20.9 %all_to_all.5 = bf16[8,8,16,256]{3,2,1,0:T(8,128)(2,1)} all-to-all(bf16[8,8,16,256]{3,2,1,0:T(8,128)(2,1)} %modes.1), channel_id=1, replica_groups=mesh['atom'=4,'tm'=8] {'tm'}, dimensions={0} | all-to-all | bytes 1048576 | tf_op jit(solution)/shard_map/all_to_all | solution.py:323
  62.8 3.8 %correlate.1 = (f32[4,16,512]{2,1,0:T(8,128)}, f32[4,16,512]{2,1,0:T(8,128)}) custom-call(bf16[64,16,256]{2,1,0:T(8,128)(2,1)} %bitcast.5), custom_call_target="tpu_custom_call" | custom-call | tf_op jit(solution)/shard_map/correlate/pallas_call | solution.py:290
  66.5 2.5 %collective-permute-start = (f32[4,16,512]{2,1,0:T(8,128)}, f32[4,16,512]{2,1,0:T(8,128)S(1)}, u32[]{:S(2)}, u32[]{:S(2)}) collective-permute-start(f32[4,16,512]{2,1,0:T(8,128)} %get-tuple-element.7), channel_id=1, source_target_pairs={{0,31},{1,30},{2,29},{3,28},{4,27},{5,26},{6,25},{7,24},{8,23},{9,... | collective-permute-start | bytes 393224 | tf_op jit(solution)/shard_map/ppermute | solution.py:325
  69.0 6.6 %collective-permute-done = f32[4,16,512]{2,1,0:T(8,128)S(1)} collective-permute-done((f32[4,16,512]{2,1,0:T(8,128)}, f32[4,16,512]{2,1,0:T(8,128)S(1)}, u32[]{:S(2)}, u32[]{:S(2)}) %collective-permute-start) | collective-permute-done | bytes 131104 | tf_op jit(solution)/shard_map/ppermute | solution.py:325
  75.6 1.6 %pad_maximum_fusion = f32[4,16,1024]{2,1,0:T(8,128)} fusion(f32[4,16,512]{2,1,0:T(8,128)} %get-tuple-element.8, f32[4,16,512]{2,1,0:T(8,128)S(1)} %collective-permute-done), kind=kLoop, calls=%fused_computation.1 | loop fusion | flops 65536 | bytes 524288 | tf_op jit(solution)/shard_map/concatenate | solution.py:326
Async XLA Ops:
  8.1 1.0 %copy-start = (s32[8,3,2048]{2,0,1:T(8,128)S(1)}, s32[8,3,2048]{2,0,1:T(8,128)}, u32[]{:S(2)}) copy-start(s32[8,3,2048]{2,0,1:T(8,128)} %param.2) | copy-start | bytes 589828
  66.5 9.1 %collective-permute-start = (f32[4,16,512]{2,1,0:T(8,128)}, f32[4,16,512]{2,1,0:T(8,128)S(1)}, u32[]{:S(2)}, u32[]{:S(2)}) collective-permute-start(f32[4,16,512]{2,1,0:T(8,128)} %get-tuple-element.7), channel_id=1, source_target_pairs={{0,31},{1,30},{2,29},{3,28},{4,27},{5,26},{6,25},{7,24},{8,23},{9,... | collective-permute-start | bytes 393224 | tf_op jit(solution)/shard_map/ppermute | solution.py:325

commit v2 on v1

v2 whole, which is shorter than its diff:
```python
import functools
import math

import jax
import jax.numpy as jnp
from jax import lax
from jax.experimental import pallas as pl
from jax.experimental.pallas import tpu as pltpu
from jax.sharding import PartitionSpec as P

KX = 32
KY = 32
KZ = 32
LAGS = 16
LATTICE = 131072
QUARTER = LATTICE // 4
HALF_Z = KZ // 2
COMPS = 4
LANES = 128
VMEM = 56 * 1024 * 1024
WIRE = jnp.bfloat16


def wave(q, extent):
    return q - extent // 2 + (1 if q >= extent // 2 else 0)


def sincos(n):
    n = jnp.bitwise_and(n, LATTICE - 1)
    quadrant = jnp.right_shift(n + QUARTER // 2, 15)
    x = (n - jnp.left_shift(quadrant, 15)).astype(jnp.float32) * (2.0 * math.pi / LATTICE)
    y = x * x
    s = y * (1.0 / 362880.0) - 1.0 / 5040.0
    s = s * y + 1.0 / 120.0
    s = s * y - 1.0 / 6.0
    s = s * y * x + x
    c = y * (1.0 / 40320.0) - 1.0 / 720.0
    c = c * y + 1.0 / 24.0
    c = c * y - 0.5
    c = c * y + 1.0
    odd = jnp.bitwise_and(quadrant, 1) == 1
    cos = jnp.where(odd, s, c)
    sin = jnp.where(odd, c, s)
    cos = jnp.where(jnp.bitwise_and(quadrant + 1, 2) == 2, -cos, cos)
    sin = jnp.where(jnp.bitwise_and(quadrant, 2) == 2, -sin, sin)
    return cos, sin


def times(a, b):
    return a[0] * b[0] - a[1] * b[1], a[0] * b[1] + a[1] * b[0]


def plus_minus(a, b):
    cc, ss, cs, sc = a[0] * b[0], a[1] * b[1], a[0] * b[1], a[1] * b[0]
    return (cc - ss, sc + cs), (cc + ss, sc - cs)


def powers(e1):
    e = {1: e1}
    e[2] = times(e1, e1)
    e[3] = times(e[2], e1)
    e[4] = times(e[2], e[2])
    e[8] = times(e[4], e[4])
    e[12], _ = plus_minus(e[8], e[4])
    for d in (1, 2, 3):
        e[8 + d], e[8 - d] = plus_minus(e[8], e[d])
    e[16] = times(e[8], e[8])
    for d in (1, 2, 3):
        _, e[16 - d] = plus_minus(e[16], e[d])
    return e


def prepare(data, slot, first_block, xs, yc, ys, zc, zs, first_w, group, y_waves):
    middle = (group - 1) // 2
    frames = data.shape[2]

    def step(i, _):
        at = pl.ds(pl.multiple_of(i * LANES, LANES), LANES)
        to = first_block + i
        n = data[slot, 0, :, at].astype(jnp.int32)
        xs[to, 0], xs[to, 1] = sincos((first_w + middle) * n)
        e1 = sincos(n)
        e = {1: e1}
        for d in range(2, group - middle):
            e[d] = times(e[d - 1], e1)
        for d in range(1, group - middle):
            xs[to, 2 * d], xs[to, 2 * d + 1] = e[d]
        e = powers(sincos(data[slot, 1, :, at].astype(jnp.int32)))
        for row, w in enumerate(y_waves):
            c, s = e[abs(w)]
            yc[to, row * frames : (row + 1) * frames, :] = c
            ys[to, row * frames : (row + 1) * frames, :] = s if w > 0 else -s
        e = powers(sincos(data[slot, 2, :, at].astype(jnp.int32)))
        for w in range(1, HALF_Z + 1):
            c, s = e[w]
            zc[to, (w - 1) * frames : w * frames, :] = c
            zs[to, (w - 1) * frames : w * frames, :] = s
        return 0

    lax.fori_loop(0, data.shape[3] // LANES, step, 0)


def frame_product(f, data, first_slot, xs, yc, ys, zc, zs, block, group, rows):
    middle = (group - 1) // 2
    frames, lanes = data.shape[2], data.shape[3]
    total = None
    steps = block // LANES

    def wide(get):
        return jnp.concatenate([get(k) for k in range(steps)], 1)

    for i in range(2 * lanes // block):
        first = i * steps
        slot, at = first_slot + i * block // lanes, pl.ds(i * block % lanes, block)

        def pick(ref):
            return wide(lambda k: ref[first + k, pl.ds(f, rows, stride=frames), :])

        y = (pick(yc), pick(ys))
        x = [wide(lambda k: xs[first + k, j, pl.ds(f, 1), :]) for j in range(2 * (group - middle))]
        mid = times((x[0], x[1]), y)
        e = {middle: mid}
        for d in range(1, group - middle):
            up, down = plus_minus(mid, (x[2 * d], x[2 * d + 1]))
            e[middle + d] = up
            if middle - d >= 0:
                e[middle - d] = down
        left = []
        for j in range(group):
            left += [e[j][0].astype(jnp.bfloat16), e[j][1].astype(jnp.bfloat16)]
        left = jnp.concatenate(left, 0)
        right = []
        for z in (pick(zc), pick(zs)):
            right.append(z.astype(jnp.bfloat16))
            for a in range(COMPS - 1):
                right.append((z * data[slot, 3 + a, pl.ds(f, 1), at]).astype(jnp.bfloat16))
        right = jnp.concatenate(right, 0)
        part = lax.dot_general(
            left, right, (((1,), (1,)), ((), ())), preferred_element_type=jnp.float32
        )
        total = part if total is None else total + part
    return total


def combine(raw, group, rows):
    lane = lax.broadcasted_iota(jnp.int32, (rows, LANES), 1)
    sign = jnp.where(lane < LANES // 2, -1.0, 1.0)
    out = []
    for j in range(group):
        re = raw[2 * j * rows : (2 * j + 1) * rows]
        im = raw[(2 * j + 1) * rows : (2 * j + 2) * rows]
        turned = pltpu.roll(im, LANES // 2, 1) * sign
        out.append(jnp.concatenate([re + turned, re - turned], 1))
    return out


def fold_matrices():
    lane = lax.broadcasted_iota(jnp.int32, (LANES, LANES), 0)
    goal = lax.broadcasted_iota(jnp.int32, (LANES, LANES), 1)
    comp = jnp.right_shift(jnp.bitwise_and(lane, 63), 4)
    step = jnp.bitwise_and(lane, HALF_Z - 1)
    own = []
    for qz in (KZ // 2 + step, KZ // 2 - 1 - step):
        own.append(comp * KZ + qz)
    mirror = [comp * KZ + KZ - 1 - (t - comp * KZ) for t in own]
    return [[(goal == t).astype(jnp.float32).astype(jnp.bfloat16) for t in side] for side in (own, mirror)]


def exact_dot(x, matrix):
    high = x.astype(jnp.bfloat16)
    low = (x - high.astype(jnp.float32)).astype(jnp.bfloat16)
    return jnp.dot(high, matrix, preferred_element_type=jnp.float32) + jnp.dot(
        low, matrix, preferred_element_type=jnp.float32
    )


def correlate(series, wide, sums, frames, rows, atoms):
    tall = min(8, rows)
    slots = 2 * (rows // tall)
    anchors = 8

    def widen(t, _):
        block = series(t).astype(jnp.float32)
        for slot in range(slots):
            r, half = divmod(slot, 2)
            wide[slot, t] = block[r * tall : (r + 1) * tall, half * LANES : (half + 1) * LANES]
        return 0

    lax.fori_loop(0, frames, widen, 0)
    for slot in range(slots):
        r, half = divmod(slot, 2)
        for t in range(LAGS):
            wide[slot, frames + t] = jnp.zeros((tall, LANES), jnp.float32)

        def step(i, acc):
            first = i * anchors
            window = [wide[slot, first + t] for t in range(LAGS)]
            for t in range(anchors):
                acc = tuple(acc[lag] + window[0] * window[lag] for lag in range(LAGS))
                window = window[1:]
                if t < anchors - 1:
                    window.append(wide[slot, first + t + LAGS])
            return acc

        zero = jnp.zeros((tall, LANES), jnp.float32)
        acc = lax.fori_loop(0, frames // anchors, step, (zero,) * LAGS)
        for lag in range(LAGS):
            sums[half, lag * rows + r * tall : lag * rows + (r + 1) * tall, :] = acc[lag] * (
                1.0 / (atoms * (frames - lag))
            )


def arrange(sums, folded, fold, out_ref, first_lane, rows, flip):
    groups = max(1, rows // 4)
    per = rows // groups
    lane = lax.broadcasted_iota(jnp.int32, (LAGS, LANES), 1)
    block = jnp.right_shift(lane, 5)
    folded[...] = exact_dot(sums[0], fold[0]) + exact_dot(sums[1], fold[1])
    for g in range(groups):
        parts = [folded[pl.ds(g * per + i, LAGS, stride=rows), :] for i in range(per)]
        if flip:
            parts = parts[::-1]
        goal = first_lane + (groups - 1 - g if flip else g) * LANES
        for c in range(COMPS):
            out = jnp.zeros((LAGS, LANES), jnp.float32)
            for i in range(per):
                shift = ((i - c) * KZ) % LANES
                part = parts[i] if shift == 0 else pltpu.roll(parts[i], shift, 1)
                out = jnp.where(block == i, part, out)
            out_ref[c, :, goal : goal + LANES] = out


def kernel(
    dims, data_ref, out_ref, data, xs, yc, ys, zc, zs, total, stage, series, wide, sums, folded,
    mirror, in_recv, x_send, relay_send, mode_send, mode_recv, mirror_send, mirror_recv,
):
    atom_ways, time_ways, y_waves, atoms = dims
    frames = data.shape[2]
    group = KX // atom_ways
    rows = KY // 2
    owned = stage.shape[2]
    split = rows // owned
    chips = atom_ways // 2
    a, t = lax.axis_index("atom"), lax.axis_index("tm")
    chip, core = a // 2, a % 2
    first = a * group
    first_w = first - KX // 2 + (first >= KX // 2).astype(jnp.int32)

    mate = (chip * 2 + 1 - core, t)
    opposite = (atom_ways - 1 - a, time_ways - 1 - t)

    def along_x(step):
        return (((chip + step) % chips) * 2 + core, t)

    def along_time(step):
        return (t + step) % time_ways

    def signal(device):
        pl.semaphore_signal(
            pltpu.get_barrier_semaphore(), inc=1, device_id=device, device_id_type=pl.DeviceIdType.MESH
        )

    def remote(src, dst, send, recv, device):
        return pltpu.make_async_remote_copy(
            src_ref=src, dst_ref=dst, send_sem=send, recv_sem=recv, device_id=device,
            device_id_type=pl.DeviceIdType.MESH,
        )

    signal(mate)
    signal(opposite)
    for step in range(1, chips):
        signal(along_x(step))
    for step in range(1, time_ways):
        signal((a, along_time(step)))

    data[0] = data_ref[...]
    total[...] = jnp.zeros_like(total)
    pl.semaphore_wait(pltpu.get_barrier_semaphore(), chips + time_ways)

    def shipped(step):
        return remote(data.at[0], data.at[2 * step], x_send.at[step], in_recv.at[2 * step], along_x(step))

    def relayed(p):
        return remote(
            data.at[2 * p], data.at[2 * p + 1], relay_send.at[p], in_recv.at[2 * p + 1], mate
        )

    def mode_copy(step, f):
        goal = along_time(step)
        return remote(
            stage.at[goal, f], series.at[t, f], mode_send.at[step, f], mode_recv.at[step, f], (a, goal)
        )

    for step in range(1, chips):
        shipped(step).start()

    def phase(p, _):
        @pl.when(p > 0)
        def _():
            shipped(p).wait_recv()

        relayed(p).start()
        prepare(data, 2 * p, 0, xs, yc, ys, zc, zs, first_w, group, y_waves)
        relayed(p).wait_recv()
        prepare(data, 2 * p + 1, data.shape[3] // LANES, xs, yc, ys, zc, zs, first_w, group, y_waves)

        def frame_step(f, _):
            total[f] += frame_product(f, data, 2 * p, xs, yc, ys, zc, zs, 4 * LANES, group, rows)

            @pl.when(p == chips - 1)
            def _():
                for j, block in enumerate(combine(total[f], group, rows)):
                    block = block.astype(stage.dtype)
                    for k in range(split):
                        stage[j * split + k, f] = block[k * owned : (k + 1) * owned]
                series[t, f] = stage[t, f]
                for step in range(1, time_ways):
                    mode_copy(step, f).start()

            return 0

        lax.fori_loop(0, frames, frame_step, 0)
        return 0

    lax.fori_loop(0, chips, phase, 0)

    def arrived(f, _):
        for step in range(1, time_ways):
            mode_copy(step, f).wait_recv()
        return 0

    lax.fori_loop(0, frames, arrived, 0)
    correlate(
        lambda u: series[u // frames, u % frames], wide, sums, time_ways * frames, owned, atoms
    )
    own_fold, mirror_fold = fold_matrices()
    arrange(sums, folded, mirror_fold, mirror, 0, owned, True)
    half = owned * KZ
    swap = remote(mirror, out_ref.at[:, :, pl.ds(0, half)], mirror_send, mirror_recv, opposite)
    swap.start()
    arrange(sums, folded, own_fold, out_ref, half, owned, False)

    def sent(f, _):
        for step in range(1, time_ways):
            mode_copy(step, f).wait_send()
        return 0

    lax.fori_loop(0, frames, sent, 0)
    for step in range(1, chips):
        shipped(step).wait_send()
    for p in range(chips):
        relayed(p).wait_send()
    swap.wait()


def call(data, atom_ways, time_ways, rows, y_waves):
    frames, lanes = data.shape[1], data.shape[2]
    atoms = lanes * atom_ways
    group = KX // atom_ways
    blocks = 2 * lanes // LANES
    tall = min(8, rows)
    dims = (atom_ways, time_ways, y_waves, atoms)
    whole = pl.BlockSpec(memory_space=pltpu.VMEM)
    dma = pltpu.SemaphoreType.DMA
    tabled = pltpu.VMEM((blocks, KY // 2 * frames, LANES), jnp.float32)
    return pl.pallas_call(
        functools.partial(kernel, dims),
        out_shape=jax.ShapeDtypeStruct((COMPS, LAGS, 2 * rows * KZ), jnp.float32),
        in_specs=[whole],
        out_specs=whole,
        scratch_shapes=[
            pltpu.VMEM((atom_ways,) + data.shape, jnp.float32),
            pltpu.VMEM((blocks, 2 * (group - (group - 1) // 2), frames, LANES), jnp.float32),
            tabled, tabled, tabled, tabled,
            pltpu.VMEM((frames, group * KY, LANES), jnp.float32),
            pltpu.VMEM((time_ways, frames, rows, 2 * LANES), WIRE),
            pltpu.VMEM((time_ways, frames, rows, 2 * LANES), WIRE),
            pltpu.VMEM((2 * (rows // tall), time_ways * frames + LAGS, tall, LANES), jnp.float32),
            pltpu.VMEM((2, LAGS * rows, LANES), jnp.float32),
            pltpu.VMEM((LAGS * rows, LANES), jnp.float32),
            pltpu.VMEM((COMPS, LAGS, rows * KZ), jnp.float32),
            dma((atom_ways,)),
            dma((atom_ways // 2,)),
            dma((atom_ways // 2,)),
            dma((time_ways, frames)),
            dma((time_ways, frames)),
            dma,
            dma,
        ],
        compiler_params=pltpu.CompilerParams(
            vmem_limit_bytes=VMEM, collective_id=0, has_side_effects=True
        ),
        name="factors",
    )(data)


def per_device(positions, velocity):
    atom_ways = lax.axis_size("atom")
    time_ways = lax.axis_size("tm")
    owned = KX * KY // (atom_ways * time_ways)
    rows = owned // 2
    y_waves = [wave(q, KY) for q in range(KY) if q % owned >= rows]
    data = jnp.concatenate([positions.astype(jnp.float32), velocity.astype(jnp.float32)], 1)
    return call(jnp.transpose(data, (1, 0, 2)), atom_ways, time_ways, rows, y_waves)


def solution(mesh):
    in_specs = (P("tm", None, "atom"), P("tm", None, "atom"))
    out_specs = P(None, None, ("atom", "tm"))
    return jax.shard_map(
        per_device, mesh=mesh, in_specs=in_specs, out_specs=out_specs, check_vma=False
    )
```

time: 77.6 us -> 48.9 us (0.63)
  blocking collectives: 38.2 us -> 0 us
  Pallas kernels: 27.3 us -> 44.9 us
  waiting for transfers between devices: 6.61 us -> 0 us
  starting transfers between devices: 2.5 us -> 0 us
  local copies, waits for them, and re-layouts: 0.02 us -> 1.68 us
  other arithmetic: 2.58 us -> 1.75 us
    all_to_all x1 -> x0, blocking collectives: 20.9 us -> none  [per_device(): lax.all_to_all(modes, 'tm', split_axis=0, concat_axis=0, tiled=True)]
    pallas_call x2 -> x1, Pallas kernels: 27.3 us -> 44.9 us  [call(): pl.pallas_call(functools.partial(kernel, dims), out_shape=jax.ShapeDtypeS...]
    all_gather x2 -> x0, blocking collectives: 17.3 us -> none  [the longest x1 9.16 us: per_device(): pos = lax.all_gather(positions, 'atom', axis=2, tiled=True)]
    ppermute x1 -> x0, waiting for transfers between devices: 6.61 us -> none  [per_device(): lax.ppermute(mirror, ('atom', 'tm'), [(b, ways - 1 - b) for b in range(wa...]
    ppermute x1 -> x0, starting transfers between devices: 2.5 us -> none  [per_device(): lax.ppermute(mirror, ('atom', 'tm'), [(b, ways - 1 - b) for b in range(wa...]
    unnamed x2 -> x3, local copies, waits for them, and re-layouts: 0.02 us -> 1.68 us
    concatenate x1 -> x0, other arithmetic: 1.63 us -> none  [per_device(): return jnp.concatenate([mirror, own], 2)]
  transfers between devices with their start and end apart: 1 -> 0, of which waited for: 1 -> 0; matrix products, arithmetic and copies ran while one was open for 0% -> 0% of each run, Pallas kernels for 0% -> 0%
where the time goes in v2:
time: 48.9 us; the launch traced here: 48.4 us
  Pallas kernels  44.9 us (92%)
  other arithmetic  1.75 us (4%)
  local copies, waits for them, and re-layouts  1.68 us (3%)
    pallas_call x1, Pallas kernels, call(): pl.pallas_call(functools.partial(kernel, dims), out_shape=jax.ShapeDtypeS...  44.9 us
    unnamed x3, local copies, waits for them, and re-layouts  1.68 us

profile of v2, /device:TPU:0, one launch (start us, length us, event | category | flops | bytes accessed | tf_op | source)
XLA Modules:
  0.0 48.4 jit_solution(1714288821798064270)
XLA Ops:
  0.0 0.0 copy-start
  0.0 1.0 %convert_element_type.6 = f32[8,3,2048]{2,0,1:T(8,128)S(1)} convert(s32[8,3,2048]{2,0,1:T(8,128)} %param.2) | non-fusion elementwise | flops 49152 | bytes 393216 | tf_op jit(solution)/shard_map/convert_element_type | solution.py:403
  1.0 0.0 copy-done
  1.0 0.8 %maximum_bitcast_fusion.data_ref = f32[6,8,2048]{2,1,0:T(8,128)} fusion(f32[8,3,2048]{2,0,1:T(8,128)S(1)} %convert_element_type.7, f32[8,3,2048]{2,0,1:T(8,128)S(1)} %convert_element_type.6), kind=kLoop, calls=%fused_computation | loop fusion | flops 98304 | bytes 786432 | tf_op jit(solution)/shard_map/transpose | solution.py:404
  1.8 44.9 %factors.1 = f32[4,16,1024]{2,1,0:T(8,128)} custom-call(f32[6,8,2048]{2,1,0:T(8,128)} %maximum_bitcast_fusion.data_ref), custom_call_target="tpu_custom_call" | custom-call | tf_op jit(solution)/shard_map/factors/pallas_call | solution.py:366
  46.7 1.7 %copy.4 = f32[4,16,1024]{2,1,0:T(8,128)} copy(f32[4,16,1024]{2,1,0:T(8,128)} %factors.1) | data formatting | bytes 524288
  (1 shorter events, 0.0 us)
Async XLA Ops:
  0.0 1.0 %copy-start = (bf16[8,3,2048]{2,0,1:T(8,128)(2,1)S(1)}, bf16[8,3,2048]{2,0,1:T(8,128)(2,1)}, u32[]{:S(2)}) copy-start(bf16[8,3,2048]{2,0,1:T(8,128)(2,1)} %param.3) | copy-start | bytes 294916

commit v3 on v2

--- a/solution.py
+++ b/solution.py
@@ -136,7 +136,7 @@
                 right.append((z * data[slot, 3 + a, pl.ds(f, 1), at]).astype(jnp.bfloat16))
         right = jnp.concatenate(right, 0)
         part = lax.dot_general(
-            left, right, (((1,), (1,)), ((), ())), preferred_element_type=jnp.float32
+            right, left, (((1,), (1,)), ((), ())), preferred_element_type=jnp.float32
         )
         total = part if total is None else total + part
     return total
@@ -309,7 +309,7 @@
 
             @pl.when(p == chips - 1)
             def _():
-                for j, block in enumerate(combine(total[f], group, rows)):
+                for j, block in enumerate(combine(jnp.transpose(total[f]), group, rows)):
                     block = block.astype(stage.dtype)
                     for k in range(split):
                         stage[j * split + k, f] = block[k * owned : (k + 1) * owned]
@@ -372,7 +372,7 @@
             pltpu.VMEM((atom_ways,) + data.shape, jnp.float32),
             pltpu.VMEM((blocks, 2 * (group - (group - 1) // 2), frames, LANES), jnp.float32),
             tabled, tabled, tabled, tabled,
-            pltpu.VMEM((frames, group * KY, LANES), jnp.float32),
+            pltpu.VMEM((frames, LANES, group * KY), jnp.float32),
             pltpu.VMEM((time_ways, frames, rows, 2 * LANES), WIRE),
             pltpu.VMEM((time_ways, frames, rows, 2 * LANES), WIRE),
             pltpu.VMEM((2 * (rows // tall), time_ways * frames + LAGS, tall, LANES), jnp.float32),

time: 48.9 us -> 49.3 us (level)
  no operation moved by 1% of the time
where the time goes in v3:
time: 49.3 us; the launch traced here: 48.7 us
  Pallas kernels  45.2 us (92%)
  other arithmetic  1.75 us (4%)
  local copies, waits for them, and re-layouts  1.68 us (3%)
    pallas_call x1, Pallas kernels, call(): pl.pallas_call(functools.partial(kernel, dims), out_shape=jax.ShapeDtypeS...  45.2 us
    unnamed x3, local copies, waits for them, and re-layouts  1.68 us

profile of v3, /device:TPU:0, one launch (start us, length us, event | category | flops | bytes accessed | tf_op | source)
XLA Modules:
  0.0 48.7 jit_solution(8107689078455103693)
XLA Ops:
  0.0 0.0 copy-start
  0.0 1.0 %convert_element_type.6 = f32[8,3,2048]{2,0,1:T(8,128)S(1)} convert(s32[8,3,2048]{2,0,1:T(8,128)} %param.2) | non-fusion elementwise | flops 49152 | bytes 393216 | tf_op jit(solution)/shard_map/convert_element_type | solution.py:403
  1.0 0.0 copy-done
  1.0 0.8 %maximum_bitcast_fusion.data_ref = f32[6,8,2048]{2,1,0:T(8,128)} fusion(f32[8,3,2048]{2,0,1:T(8,128)S(1)} %convert_element_type.7, f32[8,3,2048]{2,0,1:T(8,128)S(1)} %convert_element_type.6), kind=kLoop, calls=%fused_computation | loop fusion | flops 98304 | bytes 786432 | tf_op jit(solution)/shard_map/transpose | solution.py:404
  1.8 45.2 %factors.1 = f32[4,16,1024]{2,1,0:T(8,128)} custom-call(f32[6,8,2048]{2,1,0:T(8,128)} %maximum_bitcast_fusion.data_ref), custom_call_target="tpu_custom_call" | custom-call | tf_op jit(solution)/shard_map/factors/pallas_call | solution.py:366
  47.0 1.7 %copy.4 = f32[4,16,1024]{2,1,0:T(8,128)} copy(f32[4,16,1024]{2,1,0:T(8,128)} %factors.1) | data formatting | bytes 524288
  (1 shorter events, 0.0 us)
Async XLA Ops:
  0.0 1.0 %copy-start = (bf16[8,3,2048]{2,0,1:T(8,128)(2,1)S(1)}, bf16[8,3,2048]{2,0,1:T(8,128)(2,1)}, u32[]{:S(2)}) copy-start(bf16[8,3,2048]{2,0,1:T(8,128)(2,1)} %param.3) | copy-start | bytes 294916

commit v4 on v3

--- a/solution.py
+++ b/solution.py
@@ -74,7 +74,7 @@
     middle = (group - 1) // 2
     frames = data.shape[2]
 
-    def step(i, _):
+    def block(i):
         at = pl.ds(pl.multiple_of(i * LANES, LANES), LANES)
         to = first_block + i
         n = data[slot, 0, :, at].astype(jnp.int32)
@@ -95,12 +95,16 @@
             c, s = e[w]
             zc[to, (w - 1) * frames : w * frames, :] = c
             zs[to, (w - 1) * frames : w * frames, :] = s
+
+    def step(i, _):
+        block(2 * i)
+        block(2 * i + 1)
         return 0
 
-    lax.fori_loop(0, data.shape[3] // LANES, step, 0)
-
-
-def frame_product(f, data, first_slot, xs, yc, ys, zc, zs, block, group, rows):
+    lax.fori_loop(0, data.shape[3] // (2 * LANES), step, 0)
+
+
+def frame_product(f, data, p, xs, yc, ys, zc, zs, block, group, rows):
     middle = (group - 1) // 2
     frames, lanes = data.shape[2], data.shape[3]
     total = None
@@ -110,8 +114,8 @@
         return jnp.concatenate([get(k) for k in range(steps)], 1)
 
     for i in range(2 * lanes // block):
-        first = i * steps
-        slot, at = first_slot + i * block // lanes, pl.ds(i * block % lanes, block)
+        first = p * (2 * lanes // LANES) + i * steps
+        slot, at = 2 * p + i * block // lanes, pl.ds(i * block % lanes, block)
 
         def pick(ref):
             return wide(lambda k: ref[first + k, pl.ds(f, rows, stride=frames), :])
@@ -174,23 +178,22 @@
     )
 
 
-def correlate(series, wide, sums, frames, rows, atoms):
+def widen(series, source, wide):
+    frames, rows = series.shape[1], series.shape[2]
     tall = min(8, rows)
-    slots = 2 * (rows // tall)
+    for f in range(frames):
+        block = series[source, f].astype(jnp.float32)
+        for slot in range(wide.shape[0]):
+            r, half = divmod(slot, 2)
+            wide[slot, source * frames + f] = block[
+                r * tall : (r + 1) * tall, half * LANES : (half + 1) * LANES
+            ]
+
+
+def correlate(wide, sums, r, frames, tall, atoms):
     anchors = 8
-
-    def widen(t, _):
-        block = series(t).astype(jnp.float32)
-        for slot in range(slots):
-            r, half = divmod(slot, 2)
-            wide[slot, t] = block[r * tall : (r + 1) * tall, half * LANES : (half + 1) * LANES]
-        return 0
-
-    lax.fori_loop(0, frames, widen, 0)
-    for slot in range(slots):
-        r, half = divmod(slot, 2)
-        for t in range(LAGS):
-            wide[slot, frames + t] = jnp.zeros((tall, LANES), jnp.float32)
+    for half in range(2):
+        slot = 2 * r + half
 
         def step(i, acc):
             first = i * anchors
@@ -205,9 +208,7 @@
         zero = jnp.zeros((tall, LANES), jnp.float32)
         acc = lax.fori_loop(0, frames // anchors, step, (zero,) * LAGS)
         for lag in range(LAGS):
-            sums[half, lag * rows + r * tall : lag * rows + (r + 1) * tall, :] = acc[lag] * (
-                1.0 / (atoms * (frames - lag))
-            )
+            sums[half, lag * tall : (lag + 1) * tall, :] = acc[lag] * (1.0 / (atoms * (frames - lag)))
 
 
 def arrange(sums, folded, fold, out_ref, first_lane, rows, flip):
@@ -274,7 +275,9 @@
         signal((a, along_time(step)))
 
     data[0] = data_ref[...]
-    total[...] = jnp.zeros_like(total)
+    for slot in range(wide.shape[0]):
+        for lag in range(LAGS):
+            wide[slot, time_ways * frames + lag] = jnp.zeros(wide.shape[2:], jnp.float32)
     pl.semaphore_wait(pltpu.get_barrier_semaphore(), chips + time_ways)
 
     def shipped(step):
@@ -285,79 +288,112 @@
             data.at[2 * p], data.at[2 * p + 1], relay_send.at[p], in_recv.at[2 * p + 1], mate
         )
 
-    def mode_copy(step, f):
-        goal = along_time(step)
+    def mode_copy(step, f, count):
+        goal, at = along_time(step), pl.ds(f, count)
         return remote(
-            stage.at[goal, f], series.at[t, f], mode_send.at[step, f], mode_recv.at[step, f], (a, goal)
+            stage.at[goal, at], series.at[t, at], mode_send.at[step], mode_recv.at[step], (a, goal)
+        )
+
+    def mode_arrival(step):
+        source = (t + time_ways - step) % time_ways
+        return remote(
+            stage.at[source], series.at[source], mode_send.at[step], mode_recv.at[step], (a, source)
         )
 
     for step in range(1, chips):
         shipped(step).start()
 
-    def phase(p, _):
-        @pl.when(p > 0)
-        def _():
+    blocks = data.shape[3] // LANES
+
+    def tables(p):
+        if p > 0:
             shipped(p).wait_recv()
-
         relayed(p).start()
-        prepare(data, 2 * p, 0, xs, yc, ys, zc, zs, first_w, group, y_waves)
+        prepare(data, 2 * p, 2 * p * blocks, xs, yc, ys, zc, zs, first_w, group, y_waves)
         relayed(p).wait_recv()
-        prepare(data, 2 * p + 1, data.shape[3] // LANES, xs, yc, ys, zc, zs, first_w, group, y_waves)
-
-        def frame_step(f, _):
-            total[f] += frame_product(f, data, 2 * p, xs, yc, ys, zc, zs, 4 * LANES, group, rows)
-
-            @pl.when(p == chips - 1)
-            def _():
-                for j, block in enumerate(combine(jnp.transpose(total[f]), group, rows)):
-                    block = block.astype(stage.dtype)
-                    for k in range(split):
-                        stage[j * split + k, f] = block[k * owned : (k + 1) * owned]
-                series[t, f] = stage[t, f]
-                for step in range(1, time_ways):
-                    mode_copy(step, f).start()
-
+        prepare(data, 2 * p + 1, (2 * p + 1) * blocks, xs, yc, ys, zc, zs, first_w, group, y_waves)
+
+    def product(f, p):
+        return frame_product(f, data, p, xs, yc, ys, zc, zs, 4 * LANES, group, rows)
+
+    def emit(f):
+        for j, block in enumerate(combine(jnp.transpose(total[f]), group, rows)):
+            block = block.astype(stage.dtype)
+            for k in range(split):
+                stage[j * split + k, f] = block[k * owned : (k + 1) * owned]
+        series[t, f] = stage[t, f]
+        for step in range(1, time_ways):
+            mode_copy(step, f, 1).start()
+
+    early = frames * 5 // 8
+
+    def own_part(f, _):
+        total[f] = product(f, 0)
+        return 0
+
+    tables(0)
+    lax.fori_loop(0, early, own_part, 0)
+    for p in range(1, chips):
+        tables(p)
+
+        def far_part(f, _):
+            total[f] += product(f, p)
+            if p == chips - 1:
+                emit(f)
             return 0
 
-        lax.fori_loop(0, frames, frame_step, 0)
+        lax.fori_loop(0, early, far_part, 0)
+
+    def whole_frame(f, _):
+        total[f] = jnp.zeros(total.shape[1:], jnp.float32)
+
+        def part(p, _):
+            total[f] += product(f, p)
+            return 0
+
+        lax.fori_loop(0, chips, part, 0)
+        emit(f)
         return 0
 
-    lax.fori_loop(0, chips, phase, 0)
-
-    def arrived(f, _):
-        for step in range(1, time_ways):
-            mode_copy(step, f).wait_recv()
-        return 0
-
-    lax.fori_loop(0, frames, arrived, 0)
-    correlate(
-        lambda u: series[u // frames, u % frames], wide, sums, time_ways * frames, owned, atoms
-    )
+    lax.fori_loop(early, frames, whole_frame, 0)
+
+    widen(series, t, wide)
+    for step in range(1, time_ways):
+        mode_arrival(step).wait_recv()
+        widen(series, (t + time_ways - step) % time_ways, wide)
+
     own_fold, mirror_fold = fold_matrices()
-    arrange(sums, folded, mirror_fold, mirror, 0, owned, True)
+    tall = wide.shape[2]
     half = owned * KZ
-    swap = remote(mirror, out_ref.at[:, :, pl.ds(0, half)], mirror_send, mirror_recv, opposite)
-    swap.start()
-    arrange(sums, folded, own_fold, out_ref, half, owned, False)
-
-    def sent(f, _):
-        for step in range(1, time_ways):
-            mode_copy(step, f).wait_send()
-        return 0
-
-    lax.fori_loop(0, frames, sent, 0)
+    span = tall * KZ
+    swaps = []
+    for r in range(owned // tall):
+        correlate(wide, sums, r, time_ways * frames, tall, atoms)
+        at = half - (r + 1) * span
+        arrange(sums, folded, mirror_fold, mirror, at, tall, True)
+        swap = remote(
+            mirror.at[:, :, pl.ds(at, span)], out_ref.at[:, :, pl.ds(at, span)],
+            mirror_send.at[r], mirror_recv.at[r], opposite,
+        )
+        swap.start()
+        swaps.append(swap)
+        arrange(sums, folded, own_fold, out_ref, half + r * span, tall, False)
+
+    for step in range(1, time_ways):
+        mode_copy(step, 0, frames).wait_send()
     for step in range(1, chips):
         shipped(step).wait_send()
     for p in range(chips):
         relayed(p).wait_send()
-    swap.wait()
+    for swap in swaps:
+        swap.wait()
 
 
 def call(data, atom_ways, time_ways, rows, y_waves):
     frames, lanes = data.shape[1], data.shape[2]
     atoms = lanes * atom_ways
     group = KX // atom_ways
-    blocks = 2 * lanes // LANES
+    blocks = atom_ways * lanes // LANES
     tall = min(8, rows)
     dims = (atom_ways, time_ways, y_waves, atoms)
     whole = pl.BlockSpec(memory_space=pltpu.VMEM)
@@ -376,16 +412,16 @@
             pltpu.VMEM((time_ways, frames, rows, 2 * LANES), WIRE),
             pltpu.VMEM((time_ways, frames, rows, 2 * LANES), WIRE),
             pltpu.VMEM((2 * (rows // tall), time_ways * frames + LAGS, tall, LANES), jnp.float32),
-            pltpu.VMEM((2, LAGS * rows, LANES), jnp.float32),
-            pltpu.VMEM((LAGS * rows, LANES), jnp.float32),
+            pltpu.VMEM((2, LAGS * tall, LANES), jnp.float32),
+            pltpu.VMEM((LAGS * tall, LANES), jnp.float32),
             pltpu.VMEM((COMPS, LAGS, rows * KZ), jnp.float32),
             dma((atom_ways,)),
             dma((atom_ways // 2,)),
             dma((atom_ways // 2,)),
-            dma((time_ways, frames)),
-            dma((time_ways, frames)),
-            dma,
-            dma,
+            dma((time_ways,)),
+            dma((time_ways,)),
+            dma((rows // tall,)),
+            dma((rows // tall,)),
         ],
         compiler_params=pltpu.CompilerParams(
             vmem_limit_bytes=VMEM, collective_id=0, has_side_effects=True

time: 49.3 us -> 48.7 us (0.988)
  no operation moved by 1% of the time
where the time goes in v4:
time: 48.7 us; the launch traced here: 48.6 us
  Pallas kernels  45.1 us (93%)
  other arithmetic  1.75 us (4%)
  local copies, waits for them, and re-layouts  1.68 us (3%)
    pallas_call x1, Pallas kernels, call(): pl.pallas_call(functools.partial(kernel, dims), out_shape=jax.ShapeDtypeS...  45.1 us
    unnamed x3, local copies, waits for them, and re-layouts  1.68 us
    convert_element_type x1, other arithmetic, per_device(): positions.astype(jnp.float32)  0.97 us

profile of v4, /device:TPU:0, one launch (start us, length us, event | category | flops | bytes accessed | tf_op | source)
XLA Modules:
  0.0 48.6 jit_solution(18183109938647598190)
XLA Ops:
  0.0 0.0 copy-start
  0.0 1.0 %convert_element_type.6 = f32[8,3,2048]{2,0,1:T(8,128)S(1)} convert(s32[8,3,2048]{2,0,1:T(8,128)} %param.2) | non-fusion elementwise | flops 49152 | bytes 393216 | tf_op jit(solution)/shard_map/convert_element_type | solution.py:439
  1.0 0.0 copy-done
  1.0 0.8 %maximum_bitcast_fusion.data_ref = f32[6,8,2048]{2,1,0:T(8,128)} fusion(f32[8,3,2048]{2,0,1:T(8,128)S(1)} %convert_element_type.7, f32[8,3,2048]{2,0,1:T(8,128)S(1)} %convert_element_type.6), kind=kLoop, calls=%fused_computation | loop fusion | flops 98304 | bytes 786432 | tf_op jit(solution)/shard_map/transpose | solution.py:440
  1.8 45.1 %factors.1 = f32[4,16,1024]{2,1,0:T(8,128)} custom-call(f32[6,8,2048]{2,1,0:T(8,128)} %maximum_bitcast_fusion.data_ref), custom_call_target="tpu_custom_call" | custom-call | tf_op jit(solution)/shard_map/factors/pallas_call | solution.py:402
  46.9 1.7 %copy.4 = f32[4,16,1024]{2,1,0:T(8,128)} copy(f32[4,16,1024]{2,1,0:T(8,128)} %factors.1) | data formatting | bytes 524288
  (1 shorter events, 0.0 us)
Async XLA Ops:
  0.0 1.0 %copy-start = (bf16[8,3,2048]{2,0,1:T(8,128)(2,1)S(1)}, bf16[8,3,2048]{2,0,1:T(8,128)(2,1)}, u32[]{:S(2)}) copy-start(bf16[8,3,2048]{2,0,1:T(8,128)(2,1)} %param.3) | copy-start | bytes 294916

commit v5 on v4

--- a/solution.py
+++ b/solution.py
@@ -85,6 +85,8 @@
             e[d] = times(e[d - 1], e1)
         for d in range(1, group - middle):
             xs[to, 2 * d], xs[to, 2 * d + 1] = e[d]
+        for c in range(COMPS - 1):
+            xs[to, 2 * (group - middle) + c] = data[slot, 3 + c, :, at]
         e = powers(sincos(data[slot, 1, :, at].astype(jnp.int32)))
         for row, w in enumerate(y_waves):
             c, s = e[abs(w)]
@@ -104,43 +106,47 @@
     lax.fori_loop(0, data.shape[3] // (2 * LANES), step, 0)
 
 
-def frame_product(f, data, p, xs, yc, ys, zc, zs, block, group, rows):
+def frame_product(f, data, p, xs, yc, ys, zc, zs, lefts, rights, group, rows):
     middle = (group - 1) // 2
-    frames, lanes = data.shape[2], data.shape[3]
+    lanes = data.shape[3]
+    block = lefts.shape[2]
+    steps = block // LANES
+
+    def make(i):
+        left, right = lefts.at[i % 2], rights.at[i % 2]
+        for k in range(steps):
+            n = p * (2 * lanes // LANES) + i * steps + k
+            at = slice(k * LANES, (k + 1) * LANES)
+
+            def put(j, e):
+                for part in range(2):
+                    row = (2 * j + part) * rows
+                    left[row : row + rows, at] = e[part].astype(left.dtype)
+
+            y = (yc[n, pl.ds(f, rows, stride=data.shape[2]), :], ys[n, pl.ds(f, rows, stride=data.shape[2]), :])
+            mid = times((xs[n, 0, pl.ds(f, 1), :], xs[n, 1, pl.ds(f, 1), :]), y)
+            put(middle, mid)
+            for d in range(1, group - middle):
+                up, down = plus_minus(mid, (xs[n, 2 * d, pl.ds(f, 1), :], xs[n, 2 * d + 1, pl.ds(f, 1), :]))
+                put(middle + d, up)
+                if middle - d >= 0:
+                    put(middle - d, down)
+            u = [xs[n, 2 * (group - middle) + c, pl.ds(f, 1), :] for c in range(COMPS - 1)]
+            for part, ref in enumerate((zc, zs)):
+                z = ref[n, pl.ds(f, HALF_Z, stride=data.shape[2]), :]
+                for c in range(COMPS):
+                    row = (part * COMPS + c) * HALF_Z
+                    value = z if c == 0 else z * u[c - 1]
+                    right[row : row + HALF_Z, at] = value.astype(right.dtype)
+
+    number = 2 * lanes // block
+    make(0)
     total = None
-    steps = block // LANES
-
-    def wide(get):
-        return jnp.concatenate([get(k) for k in range(steps)], 1)
-
-    for i in range(2 * lanes // block):
-        first = p * (2 * lanes // LANES) + i * steps
-        slot, at = 2 * p + i * block // lanes, pl.ds(i * block % lanes, block)
-
-        def pick(ref):
-            return wide(lambda k: ref[first + k, pl.ds(f, rows, stride=frames), :])
-
-        y = (pick(yc), pick(ys))
-        x = [wide(lambda k: xs[first + k, j, pl.ds(f, 1), :]) for j in range(2 * (group - middle))]
-        mid = times((x[0], x[1]), y)
-        e = {middle: mid}
-        for d in range(1, group - middle):
-            up, down = plus_minus(mid, (x[2 * d], x[2 * d + 1]))
-            e[middle + d] = up
-            if middle - d >= 0:
-                e[middle - d] = down
-        left = []
-        for j in range(group):
-            left += [e[j][0].astype(jnp.bfloat16), e[j][1].astype(jnp.bfloat16)]
-        left = jnp.concatenate(left, 0)
-        right = []
-        for z in (pick(zc), pick(zs)):
-            right.append(z.astype(jnp.bfloat16))
-            for a in range(COMPS - 1):
-                right.append((z * data[slot, 3 + a, pl.ds(f, 1), at]).astype(jnp.bfloat16))
-        right = jnp.concatenate(right, 0)
+    for i in range(number):
+        if i + 1 < number:
+            make(i + 1)
         part = lax.dot_general(
-            right, left, (((1,), (1,)), ((), ())), preferred_element_type=jnp.float32
+            rights[i % 2], lefts[i % 2], (((1,), (1,)), ((), ())), preferred_element_type=jnp.float32
         )
         total = part if total is None else total + part
     return total
@@ -232,7 +238,7 @@
 
 
 def kernel(
-    dims, data_ref, out_ref, data, xs, yc, ys, zc, zs, total, stage, series, wide, sums, folded,
+    dims, data_ref, out_ref, data, xs, yc, ys, zc, zs, lefts, rights, total, stage, series, wide, sums, folded,
     mirror, in_recv, x_send, relay_send, mode_send, mode_recv, mirror_send, mirror_recv,
 ):
     atom_ways, time_ways, y_waves, atoms = dims
@@ -314,7 +320,7 @@
         prepare(data, 2 * p + 1, (2 * p + 1) * blocks, xs, yc, ys, zc, zs, first_w, group, y_waves)
 
     def product(f, p):
-        return frame_product(f, data, p, xs, yc, ys, zc, zs, 4 * LANES, group, rows)
+        return frame_product(f, data, p, xs, yc, ys, zc, zs, lefts, rights, group, rows)
 
     def emit(f):
         for j, block in enumerate(combine(jnp.transpose(total[f]), group, rows)):
@@ -406,8 +412,10 @@
         out_specs=whole,
         scratch_shapes=[
             pltpu.VMEM((atom_ways,) + data.shape, jnp.float32),
-            pltpu.VMEM((blocks, 2 * (group - (group - 1) // 2), frames, LANES), jnp.float32),
+            pltpu.VMEM((blocks, 2 * (group - (group - 1) // 2) + COMPS - 1, frames, LANES), jnp.float32),
             tabled, tabled, tabled, tabled,
+            pltpu.VMEM((2, group * KY, math.gcd(lanes, 1024)), jnp.bfloat16),
+            pltpu.VMEM((2, LANES, math.gcd(lanes, 1024)), jnp.bfloat16),
             pltpu.VMEM((frames, LANES, group * KY), jnp.float32),
             pltpu.VMEM((time_ways, frames, rows, 2 * LANES), WIRE),
             pltpu.VMEM((time_ways, frames, rows, 2 * LANES), WIRE),

time: 48.7 us -> 55.8 us (1.15)
  Pallas kernels: 45.1 us -> 52.1 us
    pallas_call x1, Pallas kernels: 45.1 us -> 52.1 us  [call(): pl.pallas_call(functools.partial(kernel, dims), out_shape=jax.ShapeDtypeS...]
where the time goes in v5:
time: 55.8 us; the launch traced here: 55.6 us
  Pallas kernels  52.1 us (93%)
  other arithmetic  1.75 us (3%)
  local copies, waits for them, and re-layouts  1.68 us (3%)
    pallas_call x1, Pallas kernels, call(): pl.pallas_call(functools.partial(kernel, dims), out_shape=jax.ShapeDtypeS...  52.1 us
    unnamed x3, local copies, waits for them, and re-layouts  1.68 us

profile of v5, /device:TPU:0, one launch (start us, length us, event | category | flops | bytes accessed | tf_op | source)
XLA Modules:
  0.0 55.6 jit_solution(7690667778877316805)
XLA Ops:
  0.0 0.0 copy-start
  0.0 1.0 %convert_element_type.6 = f32[8,3,2048]{2,0,1:T(8,128)S(1)} convert(s32[8,3,2048]{2,0,1:T(8,128)} %param.2) | non-fusion elementwise | flops 49152 | bytes 393216 | tf_op jit(solution)/shard_map/convert_element_type | solution.py:447
  1.0 0.0 copy-done
  1.0 0.8 %maximum_bitcast_fusion.data_ref = f32[6,8,2048]{2,1,0:T(8,128)} fusion(f32[8,3,2048]{2,0,1:T(8,128)S(1)} %convert_element_type.7, f32[8,3,2048]{2,0,1:T(8,128)S(1)} %convert_element_type.6), kind=kLoop, calls=%fused_computation | loop fusion | flops 98304 | bytes 786432 | tf_op jit(solution)/shard_map/transpose | solution.py:448
  1.8 52.1 %factors.1 = f32[4,16,1024]{2,1,0:T(8,128)} custom-call(f32[6,8,2048]{2,1,0:T(8,128)} %maximum_bitcast_fusion.data_ref), custom_call_target="tpu_custom_call" | custom-call | tf_op jit(solution)/shard_map/factors/pallas_call | solution.py:408
  53.9 1.7 %copy.4 = f32[4,16,1024]{2,1,0:T(8,128)} copy(f32[4,16,1024]{2,1,0:T(8,128)} %factors.1) | data formatting | bytes 524288
  (1 shorter events, 0.0 us)
Async XLA Ops:
  0.0 1.0 %copy-start = (bf16[8,3,2048]{2,0,1:T(8,128)(2,1)S(1)}, bf16[8,3,2048]{2,0,1:T(8,128)(2,1)}, u32[]{:S(2)}) copy-start(bf16[8,3,2048]{2,0,1:T(8,128)(2,1)} %param.3) | copy-start | bytes 294916

commit v6 on v4

--- a/solution.py
+++ b/solution.py
@@ -73,6 +73,7 @@
 def prepare(data, slot, first_block, xs, yc, ys, zc, zs, first_w, group, y_waves):
     middle = (group - 1) // 2
     frames = data.shape[2]
+    pitch = frames + 1
 
     def block(i):
         at = pl.ds(pl.multiple_of(i * LANES, LANES), LANES)
@@ -85,16 +86,18 @@
             e[d] = times(e[d - 1], e1)
         for d in range(1, group - middle):
             xs[to, 2 * d], xs[to, 2 * d + 1] = e[d]
+        for c in range(COMPS - 1):
+            xs[to, 2 * (group - middle) + c] = data[slot, 3 + c, :, at]
         e = powers(sincos(data[slot, 1, :, at].astype(jnp.int32)))
         for row, w in enumerate(y_waves):
             c, s = e[abs(w)]
-            yc[to, row * frames : (row + 1) * frames, :] = c
-            ys[to, row * frames : (row + 1) * frames, :] = s if w > 0 else -s
+            yc[to, row * pitch : row * pitch + frames, :] = c
+            ys[to, row * pitch : row * pitch + frames, :] = s if w > 0 else -s
         e = powers(sincos(data[slot, 2, :, at].astype(jnp.int32)))
         for w in range(1, HALF_Z + 1):
             c, s = e[w]
-            zc[to, (w - 1) * frames : w * frames, :] = c
-            zs[to, (w - 1) * frames : w * frames, :] = s
+            zc[to, (w - 1) * pitch : (w - 1) * pitch + frames, :] = c
+            zs[to, (w - 1) * pitch : (w - 1) * pitch + frames, :] = s
 
     def step(i, _):
         block(2 * i)
@@ -107,40 +110,42 @@
 def frame_product(f, data, p, xs, yc, ys, zc, zs, block, group, rows):
     middle = (group - 1) // 2
     frames, lanes = data.shape[2], data.shape[3]
+    steps = block // LANES
+
+    def make(n):
+        left = [None] * (2 * group)
+
+        def put(j, e):
+            left[2 * j], left[2 * j + 1] = e[0].astype(jnp.bfloat16), e[1].astype(jnp.bfloat16)
+
+        def row(j):
+            return xs[n, j, pl.ds(f, 1), :]
+
+        def pick(ref):
+            return ref[n, pl.ds(f, rows, stride=frames + 1), :]
+
+        mid = times((row(0), row(1)), (pick(yc), pick(ys)))
+        put(middle, mid)
+        for d in range(1, group - middle):
+            up, down = plus_minus(mid, (row(2 * d), row(2 * d + 1)))
+            put(middle + d, up)
+            if middle - d >= 0:
+                put(middle - d, down)
+        right = []
+        u = [row(2 * (group - middle) + c) for c in range(COMPS - 1)]
+        for ref in (zc, zs):
+            z = pick(ref)
+            right.append(z.astype(jnp.bfloat16))
+            right += [(z * weight).astype(jnp.bfloat16) for weight in u]
+        return jnp.concatenate(left, 0), jnp.concatenate(right, 0)
+
     total = None
-    steps = block // LANES
-
-    def wide(get):
-        return jnp.concatenate([get(k) for k in range(steps)], 1)
-
     for i in range(2 * lanes // block):
         first = p * (2 * lanes // LANES) + i * steps
-        slot, at = 2 * p + i * block // lanes, pl.ds(i * block % lanes, block)
-
-        def pick(ref):
-            return wide(lambda k: ref[first + k, pl.ds(f, rows, stride=frames), :])
-
-        y = (pick(yc), pick(ys))
-        x = [wide(lambda k: xs[first + k, j, pl.ds(f, 1), :]) for j in range(2 * (group - middle))]
-        mid = times((x[0], x[1]), y)
-        e = {middle: mid}
-        for d in range(1, group - middle):
-            up, down = plus_minus(mid, (x[2 * d], x[2 * d + 1]))
-            e[middle + d] = up
-            if middle - d >= 0:
-                e[middle - d] = down
-        left = []
-        for j in range(group):
-            left += [e[j][0].astype(jnp.bfloat16), e[j][1].astype(jnp.bfloat16)]
-        left = jnp.concatenate(left, 0)
-        right = []
-        for z in (pick(zc), pick(zs)):
-            right.append(z.astype(jnp.bfloat16))
-            for a in range(COMPS - 1):
-                right.append((z * data[slot, 3 + a, pl.ds(f, 1), at]).astype(jnp.bfloat16))
-        right = jnp.concatenate(right, 0)
+        made = [make(first + k) for k in range(steps)]
+        left, right = (jnp.concatenate(list(side), 1) for side in zip(*made))
         part = lax.dot_general(
-            right, left, (((1,), (1,)), ((), ())), preferred_element_type=jnp.float32
+            left, right, (((1,), (1,)), ((), ())), preferred_element_type=jnp.float32
         )
         total = part if total is None else total + part
     return total
@@ -317,7 +322,7 @@
         return frame_product(f, data, p, xs, yc, ys, zc, zs, 4 * LANES, group, rows)
 
     def emit(f):
-        for j, block in enumerate(combine(jnp.transpose(total[f]), group, rows)):
+        for j, block in enumerate(combine(total[f], group, rows)):
             block = block.astype(stage.dtype)
             for k in range(split):
                 stage[j * split + k, f] = block[k * owned : (k + 1) * owned]
@@ -398,7 +403,7 @@
     dims = (atom_ways, time_ways, y_waves, atoms)
     whole = pl.BlockSpec(memory_space=pltpu.VMEM)
     dma = pltpu.SemaphoreType.DMA
-    tabled = pltpu.VMEM((blocks, KY // 2 * frames, LANES), jnp.float32)
+    tabled = pltpu.VMEM((blocks, KY // 2 * (frames + 1), LANES), jnp.float32)
     return pl.pallas_call(
         functools.partial(kernel, dims),
         out_shape=jax.ShapeDtypeStruct((COMPS, LAGS, 2 * rows * KZ), jnp.float32),
@@ -406,9 +411,9 @@
         out_specs=whole,
         scratch_shapes=[
             pltpu.VMEM((atom_ways,) + data.shape, jnp.float32),
-            pltpu.VMEM((blocks, 2 * (group - (group - 1) // 2), frames, LANES), jnp.float32),
+            pltpu.VMEM((blocks, 2 * (group - (group - 1) // 2) + COMPS - 1, frames, LANES), jnp.float32),
             tabled, tabled, tabled, tabled,
-            pltpu.VMEM((frames, LANES, group * KY), jnp.float32),
+            pltpu.VMEM((frames, group * KY, LANES), jnp.float32),
             pltpu.VMEM((time_ways, frames, rows, 2 * LANES), WIRE),
             pltpu.VMEM((time_ways, frames, rows, 2 * LANES), WIRE),
             pltpu.VMEM((2 * (rows // tall), time_ways * frames + LAGS, tall, LANES), jnp.float32),

time: 48.7 us -> 46.9 us (0.963)
  Pallas kernels: 45.1 us -> 43.3 us
    pallas_call x1, Pallas kernels: 45.1 us -> 43.3 us  [call(): pl.pallas_call(functools.partial(kernel, dims), out_shape=jax.ShapeDtypeS...]
where the time goes in v6:
time: 46.9 us; the launch traced here: 46.7 us
  Pallas kernels  43.3 us (92%)
  other arithmetic  1.75 us (4%)
  local copies, waits for them, and re-layouts  1.68 us (4%)
    pallas_call x1, Pallas kernels, call(): pl.pallas_call(functools.partial(kernel, dims), out_shape=jax.ShapeDtypeS...  43.3 us
    unnamed x3, local copies, waits for them, and re-layouts  1.68 us
    convert_element_type x1, other arithmetic, per_device(): positions.astype(jnp.float32)  0.97 us

profile of v6, /device:TPU:0, one launch (start us, length us, event | category | flops | bytes accessed | tf_op | source)
XLA Modules:
  0.0 46.7 jit_solution(436522427668372040)
XLA Ops:
  0.0 0.0 copy-start
  0.0 1.0 %convert_element_type.6 = f32[8,3,2048]{2,0,1:T(8,128)S(1)} convert(s32[8,3,2048]{2,0,1:T(8,128)} %param.2) | non-fusion elementwise | flops 49152 | bytes 393216 | tf_op jit(solution)/shard_map/convert_element_type | solution.py:444
  1.0 0.0 copy-done
  1.0 0.8 %maximum_bitcast_fusion.data_ref = f32[6,8,2048]{2,1,0:T(8,128)} fusion(f32[8,3,2048]{2,0,1:T(8,128)S(1)} %convert_element_type.7, f32[8,3,2048]{2,0,1:T(8,128)S(1)} %convert_element_type.6), kind=kLoop, calls=%fused_computation | loop fusion | flops 98304 | bytes 786432 | tf_op jit(solution)/shard_map/transpose | solution.py:445
  1.8 43.3 %factors.1 = f32[4,16,1024]{2,1,0:T(8,128)} custom-call(f32[6,8,2048]{2,1,0:T(8,128)} %maximum_bitcast_fusion.data_ref), custom_call_target="tpu_custom_call" | custom-call | tf_op jit(solution)/shard_map/factors/pallas_call | solution.py:407
  45.0 1.7 %copy.4 = f32[4,16,1024]{2,1,0:T(8,128)} copy(f32[4,16,1024]{2,1,0:T(8,128)} %factors.1) | data formatting | bytes 524288
  (1 shorter events, 0.0 us)
Async XLA Ops:
  0.0 1.0 %copy-start = (bf16[8,3,2048]{2,0,1:T(8,128)(2,1)S(1)}, bf16[8,3,2048]{2,0,1:T(8,128)(2,1)}, u32[]{:S(2)}) copy-start(bf16[8,3,2048]{2,0,1:T(8,128)(2,1)} %param.3) | copy-start | bytes 294916

commit v7 on v6

--- a/solution.py
+++ b/solution.py
@@ -237,7 +237,7 @@
 
 
 def kernel(
-    dims, data_ref, out_ref, data, xs, yc, ys, zc, zs, total, stage, series, wide, sums, folded,
+    dims, pos_ref, vel_ref, out_ref, data, xs, yc, ys, zc, zs, total, stage, series, wide, sums, folded,
     mirror, in_recv, x_send, relay_send, mode_send, mode_recv, mirror_send, mirror_recv,
 ):
     atom_ways, time_ways, y_waves, atoms = dims
@@ -279,7 +279,8 @@
     for step in range(1, time_ways):
         signal((a, along_time(step)))
 
-    data[0] = data_ref[...]
+    data[0, 0:3] = pos_ref[...].astype(jnp.float32)
+    data[0, 3:6] = vel_ref[...].astype(jnp.float32)
     for slot in range(wide.shape[0]):
         for lag in range(LAGS):
             wide[slot, time_ways * frames + lag] = jnp.zeros(wide.shape[2:], jnp.float32)
@@ -319,7 +320,7 @@
         prepare(data, 2 * p + 1, (2 * p + 1) * blocks, xs, yc, ys, zc, zs, first_w, group, y_waves)
 
     def product(f, p):
-        return frame_product(f, data, p, xs, yc, ys, zc, zs, 4 * LANES, group, rows)
+        return frame_product(f, data, p, xs, yc, ys, zc, zs, min(16 * LANES, data.shape[3]), group, rows)
 
     def emit(f):
         for j, block in enumerate(combine(total[f], group, rows)):
@@ -394,8 +395,8 @@
         swap.wait()
 
 
-def call(data, atom_ways, time_ways, rows, y_waves):
-    frames, lanes = data.shape[1], data.shape[2]
+def call(positions, velocity, atom_ways, time_ways, rows, y_waves):
+    frames, lanes = positions.shape[1], positions.shape[2]
     atoms = lanes * atom_ways
     group = KX // atom_ways
     blocks = atom_ways * lanes // LANES
@@ -407,10 +408,10 @@
     return pl.pallas_call(
         functools.partial(kernel, dims),
         out_shape=jax.ShapeDtypeStruct((COMPS, LAGS, 2 * rows * KZ), jnp.float32),
-        in_specs=[whole],
+        in_specs=[whole, whole],
         out_specs=whole,
         scratch_shapes=[
-            pltpu.VMEM((atom_ways,) + data.shape, jnp.float32),
+            pltpu.VMEM((atom_ways, 6, frames, lanes), jnp.float32),
             pltpu.VMEM((blocks, 2 * (group - (group - 1) // 2) + COMPS - 1, frames, LANES), jnp.float32),
             tabled, tabled, tabled, tabled,
             pltpu.VMEM((frames, group * KY, LANES), jnp.float32),
@@ -432,7 +433,7 @@
             vmem_limit_bytes=VMEM, collective_id=0, has_side_effects=True
         ),
         name="factors",
-    )(data)
+    )(positions, velocity)
 
 
 def per_device(positions, velocity):
@@ -441,8 +442,8 @@
     owned = KX * KY // (atom_ways * time_ways)
     rows = owned // 2
     y_waves = [wave(q, KY) for q in range(KY) if q % owned >= rows]
-    data = jnp.concatenate([positions.astype(jnp.float32), velocity.astype(jnp.float32)], 1)
-    return call(jnp.transpose(data, (1, 0, 2)), atom_ways, time_ways, rows, y_waves)
+    positions, velocity = (jnp.transpose(v, (1, 0, 2)) for v in (positions, velocity))
+    return call(positions, velocity, atom_ways, time_ways, rows, y_waves)
 
 
 def solution(mesh):

time: 46.9 us -> 45.1 us (0.962)
  other arithmetic: 1.75 us -> 0 us
    convert_element_type x2 -> x0, other arithmetic: 0.99 us -> none  [the longest x1 0.97 us: per_device(): positions.astype(jnp.float32)]
    transpose x1 -> x0, other arithmetic: 0.76 us -> none  [per_device(): jnp.transpose(data, (1, 0, 2))]
    unnamed x3 -> x1, local copies, waits for them, and re-layouts: 1.68 us -> 1.67 us
where the time goes in v7:
time: 45.1 us; the launch traced here: 44.9 us
  Pallas kernels  43.2 us (96%)
  local copies, waits for them, and re-layouts  1.67 us (4%)
    pallas_call x1, Pallas kernels, call(): pl.pallas_call(functools.partial(kernel, dims), out_shape=jax.ShapeDtypeS...  43.2 us
    unnamed x1, local copies, waits for them, and re-layouts  1.67 us

profile of v7, /device:TPU:0, one launch (start us, length us, event | category | flops | bytes accessed | tf_op | source)
XLA Modules:
  0.0 44.9 jit_solution(7880670139818647785)
XLA Ops:
  0.0 43.2 %factors.1 = f32[4,16,1024]{2,1,0:T(8,128)} custom-call(s32[3,8,2048]{2,1,0:T(8,128)} %bitcast.2, bf16[3,8,2048]{2,1,0:T(8,128)(2,1)} %bitcast.3), custom_call_target="tpu_custom_call" | custom-call | tf_op jit(solution)/shard_map/factors/pallas_call | solution.py:408
  43.2 1.7 %copy.4 = f32[4,16,1024]{2,1,0:T(8,128)} copy(f32[4,16,1024]{2,1,0:T(8,128)} %factors.1) | data formatting | bytes 524288
